TPU v7x, 512 devices: a whole 4x8x8 slice. The times are simulated.
512 devices in a mesh: img: 32 (over y, z_lo, core), rows: 16 (over z_hi, x).
Axes of the slice: x: 4, y: 8, z: 8 (z_hi: 4, z_lo: 2; z = z_hi * 2 + z_lo), core: 2. Of those that a mesh axis runs over, the one named last changes fastest.
Arguments:
- center_mid: bfloat16 [32, 64, 32, 512], P('img', 'rows'), may hold values from -6 to 6
- radius_mid: bfloat16 [32, 64, 32, 512], P('img', 'rows'), may hold values from 0.049804688 to 1.5
- conv_weight: bfloat16 [512, 3, 3, 512], P('img'), may hold values from -0.09375 to 0.09375
- center_upstream: bfloat16 [32, 64, 32, 512], P('img', 'rows'), may hold values from -6 to 6
- radius_upstream: bfloat16 [32, 64, 32, 512], P('img', 'rows'), may hold values from -6 to 6
Outputs:
- center_mid_grad: bfloat16 [32, 64, 32, 512], P('img', 'rows')
- radius_mid_grad: bfloat16 [32, 64, 32, 512], P('img', 'rows')
- weight_grad: float32 [512, 3, 3, 512], P('img', None, None, 'rows')
All inputs are finite; a program needn't handle non-finite values.
Results may differ from a plain program's by a relative error of at most 0.0055.
Values may be sent and summed in bfloat16 or wider, within the bound.
A program may use at most 64 MiB of HBM per device.

v0:
```python
import jax
import jax.numpy as jnp
from jax import lax
from jax.sharding import PartitionSpec as P


def with_halo(cells, sides, width):
    for axis, dim in sides:
        count = lax.axis_size(axis)
        ends = count - 1
        head = lax.slice_in_dim(cells, 0, width, axis=dim)
        tail = lax.slice_in_dim(cells, cells.shape[dim] - width, cells.shape[dim], axis=dim)
        cells = jnp.concatenate(
            [
                lax.ppermute(tail, axis, [(i, (i + 1) % count) for i in range(ends)]),
                cells,
                lax.ppermute(head, axis, [((i + 1) % count, i) for i in range(ends)]),
            ],
            axis=dim,
        )
    return cells


def pad_columns(block):
    widths = [(0, 0)] * (block.ndim - 2) + [(1, 1), (0, 0)]
    return jnp.pad(block, widths)


def tap_product(left, kernel_tap):
    return lax.dot_general(
        left, kernel_tap, (((left.ndim - 1,), (1,)), ((), ())), preferred_element_type=jnp.float32
    )


def weight_terms(inputs_pad, piece, row_count, col_count):
    terms = []
    for tap_row in range(3):
        for tap_col in range(3):
            window = inputs_pad[
                :, :, tap_row : tap_row + row_count, tap_col : tap_col + col_count, :
            ]
            terms.append(
                lax.dot_general(
                    window,
                    piece,
                    (((1, 2, 3), (1, 2, 3)), ((0,), (0,))),
                    preferred_element_type=jnp.float32,
                )
            )
    stacked = jnp.stack(terms, axis=2)
    return stacked.reshape(stacked.shape[0], stacked.shape[1], 3, 3, stacked.shape[3])


def data_padded(padded, kernel, row_count, col_count):
    total = None
    for tap_row in range(3):
        for tap_col in range(3):
            window = padded[
                :, 2 - tap_row : 2 - tap_row + row_count, 2 - tap_col : 2 - tap_col + col_count, :
            ]
            term = tap_product(window, kernel[:, tap_row, tap_col, :])
            total = term if total is None else total + term
    return total


def layer_back(upstream, weight, inputs_pad):
    row_count = upstream.shape[2]
    col_count = upstream.shape[3]
    batch = inputs_pad.shape[1]
    kernels = (weight, jnp.abs(weight))
    operand = with_halo(upstream, (("rows", 2),), 1)
    padded = pad_columns(lax.all_gather(operand, "img", axis=1, tiled=True))
    inner = padded[:, :, 1 : row_count + 1, 1 : col_count + 1, :]
    running = weight_terms(inputs_pad, inner, row_count, col_count)
    fresh = jnp.stack(
        [data_padded(padded[which], kernels[which], row_count, col_count) for which in range(2)]
    )
    grads = fresh.astype(jnp.bfloat16)
    running, grads = (running, grads)
    image_cot = lax.all_to_all(grads, "img", split_axis=1, concat_axis=4, tiled=True)
    partial_value = (running[0] + jnp.sign(weight.astype(jnp.float32)) * running[1]) / batch
    summed = lax.psum_scatter(partial_value, "rows", scatter_dimension=3, tiled=True)
    return (image_cot, summed)


def on_device(center_mid, radius_mid, conv_weight, center_upstream, radius_upstream):
    stored = jnp.stack([center_mid, radius_mid])
    channel = lax.all_to_all(stored, "img", split_axis=4, concat_axis=1, tiled=True)
    rimmed = with_halo(channel, (("rows", 2),), 1)
    rimmed = pad_columns(rimmed)
    middle = rimmed[0].astype(jnp.float32)
    spread = rimmed[1].astype(jnp.float32)
    act_upper = jnp.maximum(middle + spread, 0.0)
    act_lower = jnp.maximum(middle - spread, 0.0)
    hidden_pad = jnp.stack([(act_upper + act_lower) * 0.5, (act_upper - act_lower) * 0.5]).astype(
        jnp.bfloat16
    )
    upstream = jnp.stack([center_upstream, radius_upstream])
    hidden_cot, weight_grad = layer_back(upstream, conv_weight, hidden_pad)
    upper_on = (center_mid > -radius_mid).astype(jnp.float32)
    lower_on = (center_mid > radius_mid).astype(jnp.float32)
    center_part = hidden_cot[0].astype(jnp.float32)
    radius_part = hidden_cot[1].astype(jnp.float32)
    upper_cot = 0.5 * (center_part + radius_part) * upper_on
    lower_cot = 0.5 * (center_part - radius_part) * lower_on
    center_mid_grad = (upper_cot + lower_cot).astype(jnp.bfloat16)
    radius_mid_grad = (upper_cot - lower_cot).astype(jnp.bfloat16)
    return (center_mid_grad, radius_mid_grad, weight_grad)


def solution(mesh):
    placed = (
        P("img", "rows", None, None),
        P("img", "rows", None, None),
        P("img", None, None, None),
        P("img", "rows", None, None),
        P("img", "rows", None, None),
    )
    return jax.shard_map(
        on_device,
        mesh=mesh,
        in_specs=placed,
        out_specs=(
            P("img", "rows", None, None),
            P("img", "rows", None, None),
            P("img", None, None, "rows"),
        ),
        check_vma=False,
    )
```

profile of v0, /device:TPU:8, one launch (start us, length us, event | category | flops | bytes accessed | tf_op | source)
XLA Modules:
  0.0 319.2 jit_solution(3447518856735842004)
XLA Ops:
  7.2 0.9 pad_maximum_fusion.6
  8.2 3.4 %collective-permute-start = (bf16[2,1,1,32,512]{4,3,2,1,0:T(8,128)(2,1)S(1)}, bf16[2,1,1,32,512]{4,3,2,1,0:T(8,128)(2,1)S(1)}, u32[]{:S(2)}, u32[]{:S(2)}) collective-permute-start(bf16[2,1,1,32,512]{4,3,2,1,0:T(8,128)(2,1)S(1)} %get-tuple-element.21), channel_id=1, source_target_pairs={{0,1},{1,2},{2,3},{3,4},{4,5},{5,6},{6,7},{7,8},{8,9},{9,10},{10,1... | collective-permute-start | bytes 196616 | tf_op jit(solution)/shard_map/ppermute | solution.py:15
  11.6 1.3 collective-permute-start.1
  12.9 0.6 collective-permute-done
  13.5 4.3 %collective-permute-done.1 = bf16[2,1,1,32,512]{4,3,2,1,0:T(8,128)(2,1)S(1)} collective-permute-done((bf16[2,1,1,32,512]{4,3,2,1,0:T(8,128)(2,1)S(1)}, bf16[2,1,1,32,512]{4,3,2,1,0:T(8,128)(2,1)S(1)}, u32[]{:S(2)}, u32[]{:S(2)}) %collective-permute-start.1) | collective-permute-done | bytes 65568 | tf_op jit(solution)/shard_map/ppermute | solution.py:17
  17.7 1.8 pad_maximum_fusion.3
  19.5 1.0 pad_maximum_fusion.4
  20.5 0.7 copy.26
  21.2 1.0 reshape.102
  22.3 20.8 %all_to_all.33 = bf16[32,2,2048]{2,1,0:T(2,128)(2,1)S(1)} all-to-all(bf16[32,2,2048]{2,1,0:T(2,128)(2,1)S(1)} %reshape.102), channel_id=1, replica_groups=mesh['img'=32,'rows'=16] {'img'}, dimensions={0} | all-to-all | bytes 524288 | tf_op jit(solution)/shard_map/all_to_all | solution.py:88
  43.1 0.5 reshape.103
  43.6 0.3 copy.91
  43.9 3.4 %collective-permute-start.2 = (bf16[2,32,1,32,16]{3,4,2,0,1:T(8,128)(2,1)S(1)}, bf16[2,32,1,32,16]{3,4,2,0,1:T(8,128)(2,1)S(1)}, u32[]{:S(2)}, u32[]{:S(2)}) collective-permute-start(bf16[2,32,1,32,16]{3,4,2,0,1:T(8,128)(2,1)S(1)} %get-tuple-element.15), channel_id=1, source_target_pairs={{0,1},{1,2},{2,3},{3,4},{4,5},{5,6},{6,7},{7,8},{8,9},{9,10},{10,1... | collective-permute-start | bytes 196616 | tf_op jit(solution)/shard_map/ppermute | solution.py:15
  47.3 1.3 collective-permute-start.3
  48.7 1.0 copy.19
  49.7 1.1 copy.20
  50.8 1.8 collective-permute-done.2
  52.6 5.7 %collective-permute-done.3 = bf16[2,32,1,32,16]{3,4,2,0,1:T(8,128)(2,1)S(1)} collective-permute-done((bf16[2,32,1,32,16]{3,4,2,0,1:T(8,128)(2,1)S(1)}, bf16[2,32,1,32,16]{3,4,2,0,1:T(8,128)(2,1)S(1)}, u32[]{:S(2)}, u32[]{:S(2)}) %collective-permute-start.3) | collective-permute-done | bytes 65568 | tf_op jit(solution)/shard_map/ppermute | solution.py:17
  58.2 0.8 fusion.43
  59.1 0.6 multiply_convert_fusion
  59.7 55.6 %all-gather.2.cloned.1.call-done = bf16[2,32,6,32,512]{4,3,2,1,0:T(8,128)(2,1)} async-done(((bf16[2,1,6,32,512]{4,3,2,1,0:T(8,128)(2,1)}), bf16[2,32,6,32,512]{4,3,2,1,0:T(8,128)(2,1)}) %all-gather.2.cloned.1.call-update) | async-done | bytes 12582928 | tf_op jit(solution)/shard_map/all_gather | solution.py:72
  115.3 11.1 %fusion = (bf16[32,6,34,512]{3,2,1,0:T(8,128)(2,1)S(1)}, bf16[32,6,34,512]{3,2,1,0:T(8,128)(2,1)S(1)}) fusion(bf16[2,32,6,32,512]{4,3,2,1,0:T(8,128)(2,1)} %all-gather.2.cloned.1.call-done), kind=kLoop, calls=%fused_computation.2 | loop fusion | bytes 25952256 | tf_op jit(solution)/shard_map/squeeze | solution.py:76
  126.4 2.8 fusion.34
  129.2 2.8 fusion.28
  132.1 2.8 fusion.30
  134.9 2.8 fusion.22
  137.8 2.8 fusion.24
  140.6 3.0 fusion.16
  143.6 2.8 fusion.10
  146.5 2.8 fusion.12
  149.3 2.8 fusion.4
  152.2 2.8 fusion.6
  155.0 2.9 fusion.88
  157.9 3.2 %fusion.85 = f32[32,4,32,16]{2,3,1,0:T(8,128)S(1)} fusion(f32[32,4,32,16]{2,3,1,0:T(8,128)S(1)} %fusion.28, f32[32,4,32,16]{2,3,1,0:T(8,128)S(1)} %fusion.30, f32[32,4,32,16]{2,3,1,0:T(8,128)S(1)} %fusion.88, bf16[32,6,34,512]{3,2,1,0:T(8,128)(2,1)S(1)} %get-tuple-element.9, bf16[16,3,3,512]{3,0,2,1:T(8,128)(2,1)S(1)} %copy-done.2), kind=kOutput, calls=%fused_computation.83 | convolution fusion | flops 67305472 | bytes 7618560 | tf_op jit(solution)/shard_map/dot_general | solution.py:30
  161.1 2.9 fusion.79
  164.0 2.8 fusion.100
  166.8 2.8 fusion.91
  169.7 2.9 fusion.73
  172.6 2.9 fusion.67
  175.5 2.9 fusion.103
  178.3 0.3 copy_bitcast_fusion.1
  178.6 1.7 reshape.100
  180.4 5.5 %all-to-all-start = ((bf16[32,2,2048]{2,1,0:T(2,128)(2,1)}), bf16[32,2,2048]{2,1,0:T(2,128)(2,1)}, u32[]{:S(2)}, u32[]{:S(2)}) async-start(bf16[32,2,2048]{2,1,0:T(2,128)(2,1)} %reshape.100), calls=%async_computation | async-start | bytes 524288 | tf_op jit(solution)/shard_map/all_to_all | solution.py:80
  185.9 4.6 %fusion.114 = f32[2,16,9,512]{3,1,0,2:T(8,128)S(1)} fusion(bf16[1,32,6,34,16]{3,4,2,0,1:T(8,128)(2,1)S(1)} %get-tuple-element.14, bf16[1,32,6,34,16]{3,4,2,0,1:T(8,128)(2,1)S(1)} %get-tuple-element.13, bf16[2,32,6,32,512]{4,3,2,1,0:T(8,128)(2,1)} %all-gather.2.cloned.1.call-done), kind=kOutput, calls=%fused_computation.109 | convolution fusion | flops 134348800 | bytes 8871936 | tf_op jit(solution)/shard_map/dot_general | solution.py:43
  190.5 4.9 %fusion.113 = f32[2,16,9,512]{3,1,0,2:T(8,128)S(1)} fusion(f32[2,16,9,512]{3,1,0,2:T(8,128)S(1)} %fusion.114, bf16[1,32,6,34,16]{3,4,2,0,1:T(8,128)(2,1)S(1)} %get-tuple-element.14, bf16[1,32,6,34,16]{3,4,2,0,1:T(8,128)(2,1)S(1)} %get-tuple-element.13, bf16[2,32,6,32,512]{4,3,2,1,0:T(8,128)(2,1)} %all-gather.2.cloned.1.call-done), kind=kOutput, calls=%fused_computation.107 | convolution fusion | flops 134348800 | bytes 10027008 | tf_op jit(solution)/shard_map/dot_general | solution.py:43
  195.4 0.3 slice-done.2
  195.7 1.9 fusion.112
  197.6 1.4 fusion.111
  199.0 1.9 fusion.110
  200.9 1.9 fusion.109
  202.8 1.5 fusion.108
  204.3 1.9 fusion.107
  206.2 1.9 fusion.106
  208.2 1.5 copy.69
  209.7 2.1 reshape.98
  211.9 2.0 reshape.101
  213.9 0.3 bitcast_bitcast_fusion
  214.2 0.3 fusion.115
  214.7 0.4 subtract_convert_fusion
  215.1 0.8 copy.38
  216.0 0.8 copy.39
  216.8 93.7 %reduce-scatter.4.cloned.1.call-done = f32[32,144]{1,0:T(8,128)} async-done(((f32[512,144]{1,0:T(8,128)}), f32[32,144]{1,0:T(8,128)}) %reduce-scatter.4.cloned.1.call-update) | async-done | bytes 18448
  310.6 0.9 reshape.99
  311.4 0.8 copy.70
  (27 shorter events, 0.5 us)
Async XLA Ops:
  7.2 42.5 %copy-start.4 = (bf16[1,4,32,512]{3,2,1,0:T(8,128)(2,1)S(1)}, bf16[1,4,32,512]{3,2,1,0:T(8,128)(2,1)}, u32[]{:S(2)}) copy-start(bf16[1,4,32,512]{3,2,1,0:T(8,128)(2,1)} %param.5) | copy-start | bytes 393220
  7.2 41.5 %copy-start.3 = (bf16[1,4,32,512]{3,2,1,0:T(8,128)(2,1)S(1)}, bf16[1,4,32,512]{3,2,1,0:T(8,128)(2,1)}, u32[]{:S(2)}) copy-start(bf16[1,4,32,512]{3,2,1,0:T(8,128)(2,1)} %param.6) | copy-start | bytes 393220
  7.2 43.5 %copy-start.2 = (bf16[16,3,3,512]{3,0,2,1:T(8,128)(2,1)S(1)}, bf16[16,3,3,512]{3,0,2,1:T(8,128)(2,1)}, u32[]{:S(2)}) copy-start(bf16[16,3,3,512]{3,0,2,1:T(8,128)(2,1)} %param.7) | copy-start | bytes 442372
  7.2 108.1 %all-gather.2.cloned.1.call-start = ((), (), s32[]{:S(2)}) async-start(), calls=%async_computation.3 | async-start | bytes 12976128 | tf_op jit(solution)/shard_map/all_gather | solution.py:72
  8.2 5.3 %collective-permute-start = (bf16[2,1,1,32,512]{4,3,2,1,0:T(8,128)(2,1)S(1)}, bf16[2,1,1,32,512]{4,3,2,1,0:T(8,128)(2,1)S(1)}, u32[]{:S(2)}, u32[]{:S(2)}) collective-permute-start(bf16[2,1,1,32,512]{4,3,2,1,0:T(8,128)(2,1)S(1)} %get-tuple-element.21), channel_id=1, source_target_pairs={{0,1},{1,2},{2,3},{3,4},{4,5},{5,6},{6,7},{7,8},{8,9},{9,10},{10,1... | collective-permute-start | bytes 196616 | tf_op jit(solution)/shard_map/ppermute | solution.py:15
  11.6 6.2 %collective-permute-start.1 = (bf16[2,1,1,32,512]{4,3,2,1,0:T(8,128)(2,1)S(1)}, bf16[2,1,1,32,512]{4,3,2,1,0:T(8,128)(2,1)S(1)}, u32[]{:S(2)}, u32[]{:S(2)}) collective-permute-start(bf16[2,1,1,32,512]{4,3,2,1,0:T(8,128)(2,1)S(1)} %get-tuple-element.22), channel_id=1, source_target_pairs={{1,0},{2,1},{3,2},{4,3},{5,4},{6,5},{7,6},{8,7},{9,8},{10,9},{11,1... | collective-permute-start | bytes 196616 | tf_op jit(solution)/shard_map/ppermute | solution.py:17
  43.9 8.7 %collective-permute-start.2 = (bf16[2,32,1,32,16]{3,4,2,0,1:T(8,128)(2,1)S(1)}, bf16[2,32,1,32,16]{3,4,2,0,1:T(8,128)(2,1)S(1)}, u32[]{:S(2)}, u32[]{:S(2)}) collective-permute-start(bf16[2,32,1,32,16]{3,4,2,0,1:T(8,128)(2,1)S(1)} %get-tuple-element.15), channel_id=1, source_target_pairs={{0,1},{1,2},{2,3},{3,4},{4,5},{5,6},{6,7},{7,8},{8,9},{9,10},{10,1... | collective-permute-start | bytes 196616 | tf_op jit(solution)/shard_map/ppermute | solution.py:15
  47.3 10.9 %collective-permute-start.3 = (bf16[2,32,1,32,16]{3,4,2,0,1:T(8,128)(2,1)S(1)}, bf16[2,32,1,32,16]{3,4,2,0,1:T(8,128)(2,1)S(1)}, u32[]{:S(2)}, u32[]{:S(2)}) collective-permute-start(bf16[2,32,1,32,16]{3,4,2,0,1:T(8,128)(2,1)S(1)} %get-tuple-element.16), channel_id=1, source_target_pairs={{1,0},{2,1},{3,2},{4,3},{5,4},{6,5},{7,6},{8,7},{9,8},{10,9},{11,1... | collective-permute-start | bytes 196616 | tf_op jit(solution)/shard_map/ppermute | solution.py:17
  180.4 31.5 %all-to-all-start = ((bf16[32,2,2048]{2,1,0:T(2,128)(2,1)}), bf16[32,2,2048]{2,1,0:T(2,128)(2,1)}, u32[]{:S(2)}, u32[]{:S(2)}) async-start(bf16[32,2,2048]{2,1,0:T(2,128)(2,1)} %reshape.100), calls=%async_computation | async-start | bytes 524288 | tf_op jit(solution)/shard_map/all_to_all | solution.py:80
  185.9 124.7 %reduce-scatter.4.cloned.1.call-start = ((), (), s32[]{:S(2)}) async-start(), calls=%async_computation.4 | async-start | bytes 557056
  185.9 9.5 %slice-start = ((s8[12582912]{0:T(1024)(128)(4,1)}), s8[4194304]{0:T(1024)(128)(4,1)S(1)}, s32[]{:S(2)}) async-start(s8[12582912]{0:T(1024)(128)(4,1)} %bitcast.233), calls=%async_computation.5 | async-start | bytes 8388608
  185.9 9.5 %slice-start.1 = ((s8[12582912]{0:T(1024)(128)(4,1)}), s8[4194304]{0:T(1024)(128)(4,1)S(1)}, s32[]{:S(2)}) async-start(s8[12582912]{0:T(1024)(128)(4,1)} %bitcast.233), calls=%async_computation.6 | async-start | bytes 8388608
  190.5 5.2 %slice-start.2 = ((s8[12582912]{0:T(1024)(128)(4,1)}), s8[4194304]{0:T(1024)(128)(4,1)S(1)}, s32[]{:S(2)}) async-start(s8[12582912]{0:T(1024)(128)(4,1)} %bitcast.233), calls=%async_computation.7 | async-start | bytes 8388608
  211.8 2.9 copy-start
  211.8 2.9 copy-start.1
Sparse Core Ops, SparseCore 0:
  19.7 95.5 all-gather.1
  212.0 98.5 reduce-scatter.3
where the time goes:
time: 325 us; the launch traced here: 319 us
  waiting for transfers between devices  162 us (50%)
  matrix products  73.7 us (23%)
  local copies, waits for them, and re-layouts  27.2 us (8%)
  blocking collectives  20.8 us (6%)
  starting transfers between devices  15 us (5%)
  between operations  14.5 us (4%)
  other arithmetic  6.35 us (2%)
    unnamed x3, waiting for transfers between devices  93.8 us
    all_gather x1, waiting for transfers between devices, layer_back(): padded = pad_columns(lax.all_gather(operand, 'img', axis=1, tiled=True))  55.6 us
    dot_general x18, matrix products, tap_product(): lax.dot_general(left, kernel_tap, (((left.ndim - 1,), (1,)), ((), ())), p...  51.9 us
    dot_general x9, matrix products, weight_terms(): lax.dot_general(window, piece, (((1, 2, 3), (1, 2, 3)), ((0,), (0,))), pr...  21.8 us
    all_to_all x1, blocking collectives, on_device(): lax.all_to_all(stored, 'img', split_axis=4, concat_axis=1, tiled=True)  20.8 us
    unnamed x28, local copies, waits for them, and re-layouts  14.6 us
    squeeze x1, local copies, waits for them, and re-layouts, layer_back(): padded[which]  11.1 us
    ppermute x2, waiting for transfers between devices, with_halo(): lax.ppermute(head, axis, [((i + 1) % count, i) for i in range(ends)])  9.94 us
  transfers between devices with their start and end apart: 7, of which 6 were waited for; matrix products, arithmetic and copies ran while one was open for 12% of the time, Pallas kernels for 0%

commit v1 on v0

v1 whole, which is shorter than its diff:
```python
import jax
import jax.numpy as jnp
from jax import lax
from jax.experimental import pallas as pl
from jax.experimental.pallas import tpu as pltpu
from jax.sharding import PartitionSpec as P

MESH = pl.DeviceIdType.MESH
F32 = jnp.float32
BF16 = jnp.bfloat16


def place(x, y, z, c):
    return ((y * 2 + lax.rem(z, 2)) * 2 + c, (z // 2) * 4 + x)


def remote(src, dst, send, recv, where):
    return pltpu.make_async_remote_copy(
        src_ref=src, dst_ref=dst, send_sem=send, recv_sem=recv, device_id=where, device_id_type=MESH
    )


def mul(value, by):
    return pl.multiple_of(value, by)


def kernel(
    cm_hbm, rm_hbm, gc_hbm, gr_hbm, w_ref,
    cm_out, rm_out, wg_out,
    cm, rm, vsend, vbuf, vt, gbuf, wbuf, acc, rs_out, rs_in, b_out, b_in, halo_out, halo_in, total, r_out, r_in,
    load_sem, gload_sem, v_send, v_recv, vh_send, vh_recv, g_send, g_recv, p_send, p_recv,
    w_send, w_recv, wz_send, wz_recv, rs_send, rs_recv, b_send, b_recv, h_send, h_recv, r_send, r_recv,
):
    i_img, i_rows = lax.axis_index("img"), lax.axis_index("rows")
    x, z_hi = lax.rem(i_rows, 4), i_rows // 4
    y, z_lo, c = i_img // 4, lax.rem(i_img // 2, 2), lax.rem(i_img, 2)
    z = z_hi * 2 + z_lo
    block = x + 4 * c
    w_source = lax.rem(y, 4) == x
    w_core = y // 4
    part_core, part_half = z // 4, lax.rem(z // 2, 2)

    load_cm = pltpu.make_async_copy(cm_hbm, cm, load_sem.at[0])
    load_rm = pltpu.make_async_copy(rm_hbm, rm, load_sem.at[1])
    load_cm.start()
    load_rm.start()
    own_rows = pl.ds(mul(64 + 128 * x, 64), 128)

    def g_load(q, arr, ref):
        return pltpu.make_async_copy(
            ref.at[:, pl.ds(mul(128 * q, 128), 128)], gbuf.at[q, arr, c, own_rows], gload_sem.at[q, arr]
        )

    for q in range(4):
        g_load(q, 0, gc_hbm).start()
        g_load(q, 1, gr_hbm).start()

    barrier = pltpu.get_barrier_semaphore()

    def greet(where):
        pl.semaphore_signal(barrier, inc=1, device_id=where, device_id_type=MESH)

    def greet_ring(k, _):
        xd, cd = lax.rem(x + lax.rem(k, 4), 4), lax.rem(c + k // 4, 2)
        greet(place(xd, y, z, cd))
        return 0

    lax.fori_loop(1, 8, greet_ring, 0)

    def greet_z(k, _):
        greet(place(x, y, lax.rem(z + k, 8), c))
        return 0

    lax.fori_loop(1, 8, greet_z, 0)
    for cf in range(2):
        @pl.when(jnp.logical_or(y != block, c != cf))
        def _():
            greet(place(x, block, z, cf))

    b_self = jnp.logical_and(y == block, part_core == c)

    def greet_b(k, _):
        ys, half = k // 2, lax.rem(k, 2)
        xs, cs, zs = lax.rem(y, 4), y // 4, 2 * (2 * c + half) + z_lo
        same = (xs == x) & (ys == y) & (zs == z) & (cs == c)

        @pl.when(jnp.logical_not(same))
        def _():
            greet(place(xs, ys, zs, cs))
        return 0

    lax.fori_loop(0, 16, greet_b, 0)
    expected = (
        30
        + jnp.where(w_source, 8 - jnp.where(c == w_core, 1, 0), 0)
        - jnp.where(b_self, 1, 0)
    )

    zero_rows = jnp.zeros((64, 128), BF16)

    def clear(q, _):
        for arr in range(2):
            for image in range(2):
                gbuf[q, arr, image, 0:64, :] = zero_rows
                gbuf[q, arr, image, 576:640, :] = zero_rows
        return 0

    lax.fori_loop(0, 4, clear, 0)

    load_cm.wait()
    load_rm.wait()
    lane = lax.broadcasted_iota(jnp.int32, (128, 128), 1)
    for j in range(4):
        middle = cm[:, 128 * j : 128 * j + 128].astype(F32)
        spread = rm[:, 128 * j : 128 * j + 128].astype(F32)
        upper = jnp.maximum(middle + spread, 0.0)
        lower = jnp.maximum(middle - spread, 0.0)
        center = (upper + lower) * 0.5
        radius = (upper - lower) * 0.5
        vsend[2 * j] = jnp.where(lane < 64, center, pltpu.roll(radius, 64, 1)).astype(BF16)
        vsend[2 * j + 1] = jnp.where(lane < 64, pltpu.roll(center, 64, 1), radius).astype(BF16)

    pl.semaphore_wait(barrier, expected)

    def v_rows(xs):
        return pl.ds(mul(32 + 128 * xs, 32), 128)

    def v_copy(b):
        return remote(
            vsend.at[b], vbuf.at[c, v_rows(x)], v_send.at[b], v_recv.at[block],
            place(lax.rem(b, 4), y, z, b // 4),
        )

    def v_own():
        return pltpu.make_async_copy(vsend.at[block], vbuf.at[c, v_rows(x)], v_recv.at[block])

    v_own().start()

    def v_start(k, _):
        v_copy(lax.rem(block + k, 8)).start()
        return 0

    lax.fori_loop(1, 8, v_start, 0)

    def g_copy(q, xd):
        return remote(
            gbuf.at[q, :, c, own_rows], gbuf.at[q, :, c, own_rows], g_send.at[q, xd], g_recv.at[q, x],
            place(xd, y, z, c),
        )

    own_shard = z_lo * 2 + c

    def w_copy(q, yd):
        return remote(
            w_ref.at[q], wbuf.at[q, :, own_shard], w_send.at[q, yd], w_recv.at[q, c],
            place(x, yd, z, w_core),
        )

    def w_own(q):
        return pltpu.make_async_copy(w_ref.at[q], wbuf.at[q, :, own_shard], w_recv.at[q, c])

    def start_q(q, _):
        g_load(q, 0, gc_hbm).wait()
        g_load(q, 1, gr_hbm).wait()
        for k in range(1, 4):
            g_copy(q, lax.rem(x + k, 4)).start()

        @pl.when(w_source)
        def _():
            def to_y(k, _):
                w_copy(q, lax.rem(y + k, 8)).start()
                return 0

            lax.fori_loop(1, 8, to_y, 0)

            @pl.when(c == w_core)
            def _():
                w_own(q).start()

            @pl.when(c != w_core)
            def _():
                w_copy(q, y).start()
        return 0

    lax.fori_loop(0, 4, start_q, 0)

    for arr in range(2):
        acc[arr] = jnp.zeros((1152, 256), F32)

    def v_wait(b, _):
        pltpu.make_async_copy(vsend.at[b], vbuf.at[b // 4, v_rows(lax.rem(b, 4))], v_recv.at[b]).wait()
        return 0

    lax.fori_loop(0, 8, v_wait, 0)
    down, up = z_hi > 0, z_hi < 3
    z_down, z_up = lax.rem(z + 6, 8), lax.rem(z + 2, 8)
    vh_down = remote(
        vbuf.at[:, 32:64], vbuf.at[:, 544:576], vh_send.at[0], vh_recv.at[0], place(x, y, z_down, c)
    )
    vh_up = remote(
        vbuf.at[:, 512:544], vbuf.at[:, 0:32], vh_send.at[1], vh_recv.at[1], place(x, y, z_up, c)
    )

    @pl.when(down)
    def _():
        vh_down.start()

    @pl.when(up)
    def _():
        vh_up.start()

    def p_copy(q):
        ring_rows = gbuf.at[q, :, c, 64:576]
        return remote(ring_rows, ring_rows, p_send.at[q], p_recv.at[q], place(x, y, z, 1 - c))

    def p_wait(q):
        got = gbuf.at[q, :, 1 - c, 64:576]
        remote(got, got, p_send.at[q], p_recv.at[q], place(x, y, z, 1 - c)).wait_recv()

    ahead = lax.rem(z_lo + c, 2) == 0
    z_mate = lax.rem(jnp.where(ahead, z + 1, z + 7), 8)

    def wz_copy(q):
        half = wbuf.at[q, :, pl.ds(z_lo * 2, 2)]
        return remote(half, half, wz_send.at[q], wz_recv.at[q], place(x, y, z_mate, c))

    def wz_wait(q):
        half = wbuf.at[q, :, pl.ds((1 - z_lo) * 2, 2)]
        remote(half, half, wz_send.at[q], wz_recv.at[q], place(x, y, z_mate, c)).wait_recv()

    def forward(q):
        for k in range(1, 4):
            xs = lax.rem(x + k, 4)
            got = gbuf.at[q, :, c, pl.ds(mul(64 + 128 * xs, 64), 128)]
            remote(got, got, g_send.at[q, xs], g_recv.at[q, xs], place(xs, y, z, c)).wait_recv()
        p_copy(q).start()
        for cf in range(2):
            got = wbuf.at[q, :, z_lo * 2 + cf]
            pltpu.make_async_copy(w_ref.at[q], got, w_recv.at[q, cf]).wait()
        wz_copy(q).start()

    forward(0)

    @pl.when(down)
    def _():
        vh_up.wait_recv()

    @pl.when(up)
    def _():
        vh_down.wait_recv()

    @pl.when(jnp.logical_not(down))
    def _():
        vbuf[:, 0:32, :] = jnp.zeros((2, 32, 128), BF16)

    @pl.when(jnp.logical_not(up))
    def _():
        vbuf[:, 544:576, :] = jnp.zeros((2, 32, 128), BF16)

    column = lax.broadcasted_iota(jnp.int32, (64, 128), 0) & 31

    def turn(piece, _):
        vals = []
        for part in range(2):
            at = piece * 2 + part
            image, row = at // 9, lax.rem(at, 9)
            vals.append(vbuf[image, pl.ds(mul(row * 64, 64), 64), :].astype(F32))
        taps = [
            [jnp.where(column == 0, 0.0, pltpu.roll(v, 1, 0)) for v in vals],
            vals,
            [jnp.where(column == 31, 0.0, pltpu.roll(v, 63, 0)) for v in vals],
        ]
        for tap in range(3):
            turned = jnp.concatenate(taps[tap], axis=0).T.astype(BF16)
            for arr in range(2):
                vt[arr, tap * 64 : tap * 64 + 64, pl.ds(mul(piece * 128, 128), 128)] = turned[
                    arr * 64 : arr * 64 + 64
                ]
        return 0

    lax.fori_loop(0, 9, turn, 0)

    def rs_copy(q, zd):
        return remote(
            rs_out.at[q, zd], rs_in.at[q, z], rs_send.at[q, zd], rs_recv.at[q, z], place(x, y, zd, c)
        )

    def b_place(q, xf):
        return place(xf, block, 2 * q + z_lo, part_core)

    def b_is_self(q, xf):
        return (xf == x) & b_self & (q == z_hi)

    def b_copy(q, xf):
        return remote(
            b_out.at[q], b_in.at[y, part_half], b_send.at[q, xf], b_recv.at[y, part_half], b_place(q, xf)
        )

    def reduce_z(q):
        def one(zs, _):
            pltpu.make_async_copy(rs_out.at[q, zs], rs_in.at[q, zs], rs_recv.at[q, zs]).wait()
            return 0

        lax.fori_loop(0, 8, one, 0)
        value = rs_in[q, 0].astype(F32)
        for zs in range(1, 8):
            value = value + rs_in[q, zs].astype(F32)
        b_out[q] = value.astype(BF16)
        for k in range(4):
            xf = lax.rem(x + k, 4)

            @pl.when(b_is_self(q, xf))
            def _():
                pltpu.make_async_copy(
                    b_out.at[q], b_in.at[y, part_half], b_recv.at[y, part_half]
                ).start()

            @pl.when(jnp.logical_not(b_is_self(q, xf)))
            def _():
                b_copy(q, xf).start()

    def step(q, _):
        p_wait(q)
        wz_wait(q)
        kern = wbuf[q].reshape(192, 384)
        kern_abs = jnp.abs(kern)
        windows = []
        for arr in range(2):
            views = []
            for image in range(2):
                views.append(
                    jnp.concatenate(
                        [gbuf[q, arr, image, 64 - 32 * a : 640 - 32 * a, :] for a in range(3)], axis=1
                    )
                )
            windows.append(jnp.concatenate(views, axis=0))
        terms = [
            jnp.dot(vt[arr], windows[arr], preferred_element_type=F32) for arr in range(2)
        ]
        wide = kern.astype(F32)
        signed = jnp.where(wide > 0, terms[1], jnp.where(wide < 0, -terms[1], 0.0))
        partial = (terms[0] + signed).astype(BF16)
        for zd in range(8):
            shard, half = (zd % 2) * 2 + zd // 4, (zd // 2) % 2
            for k in range(5):
                a, tap = divmod(4 * half + k, 3)
                rs_out[q, zd, 16 * k : 16 * k + 16, :] = partial[
                    tap * 64 + shard * 16 : tap * 64 + shard * 16 + 16, a * 128 : a * 128 + 128
                ]
        pltpu.make_async_copy(rs_out.at[q, z], rs_in.at[q, z], rs_recv.at[q, z]).start()

        def rs_start(k, _):
            rs_copy(q, lax.rem(z + k, 8)).start()
            return 0

        lax.fori_loop(1, 8, rs_start, 0)
        for arr, factor in ((0, kern), (1, kern_abs)):
            acc[arr, :, 0:192] += lax.dot_general(
                windows[arr], factor, (((1,), (1,)), ((), ())), preferred_element_type=F32
            )

        @pl.when(q < 3)
        def _():
            forward(q + 1)

        @pl.when(q > 0)
        def _():
            reduce_z(q - 1)
        return 0

    lax.fori_loop(0, 4, step, 0)

    lane64 = lax.broadcasted_iota(jnp.int32, (64, 128), 1) < 64

    def fold(k, _):
        rows = pl.ds(mul(k * 64, 64), 64)
        c01, r01 = acc[0, rows, 0:128], acc[1, rows, 0:128]
        c2, r2 = acc[0, rows, 128:256], acc[1, rows, 128:256]
        first = jnp.where(lane64, c01, pltpu.roll(r01, 64, 1))
        middle = jnp.where(lane64, pltpu.roll(c01, 64, 1), r01)
        last = jnp.where(lane64, c2, pltpu.roll(r2, 64, 1))
        total[rows, :] = (
            middle
            + jnp.where(column == 31, 0.0, pltpu.roll(first, 63, 0))
            + jnp.where(column == 0, 0.0, pltpu.roll(last, 1, 0))
        )
        return 0

    lax.fori_loop(0, 18, fold, 0)
    for image in range(2):
        halo_out[0, image] = total[576 * image : 576 * image + 32, :]
        halo_out[1, image] = total[576 * image + 544 : 576 * image + 576, :]
    h_down = remote(halo_out.at[0], halo_in.at[0], h_send.at[0], h_recv.at[0], place(x, y, z_down, c))
    h_up = remote(halo_out.at[1], halo_in.at[1], h_send.at[1], h_recv.at[1], place(x, y, z_up, c))

    @pl.when(down)
    def _():
        h_down.start()

    @pl.when(up)
    def _():
        h_up.start()

    for image in range(2):
        r_out[image] = total[576 * image + 32 : 576 * image + 544, :].astype(BF16)

    def r_copy(b):
        return remote(
            r_out.at[b // 4, pl.ds(mul(128 * lax.rem(b, 4), 128), 128)], r_in.at[block],
            r_send.at[b], r_recv.at[block], place(lax.rem(b, 4), y, z, b // 4),
        )

    def r_send_to(b):
        @pl.when(b == block)
        def _():
            pltpu.make_async_copy(
                r_out.at[c, pl.ds(mul(128 * x, 128), 128)], r_in.at[block], r_recv.at[block]
            ).start()

        @pl.when(b != block)
        def _():
            r_copy(b).start()

    for b in (1, 2, 5, 6):
        r_send_to(b)
    reduce_z(3)

    @pl.when(up)
    def _():
        h_down.wait_recv()
        for image in range(2):
            r_out[image, 480:512, :] = (total[576 * image + 512 : 576 * image + 544, :] + halo_in[0, image]).astype(BF16)

    @pl.when(down)
    def _():
        h_up.wait_recv()
        for image in range(2):
            r_out[image, 0:32, :] = (total[576 * image + 32 : 576 * image + 64, :] + halo_in[1, image]).astype(BF16)

    for b in (0, 3, 4, 7):
        r_send_to(b)

    def r_wait(b, _):
        pltpu.make_async_copy(r_out.at[0, 0:128], r_in.at[b], r_recv.at[b]).wait()
        return 0

    lax.fori_loop(0, 8, r_wait, 0)
    low = lane < 64
    for j in range(4):
        lanes = slice(128 * j, 128 * j + 128)
        even, odd = r_in[2 * j].astype(F32), r_in[2 * j + 1].astype(F32)
        center = jnp.where(low, even, pltpu.roll(odd, 64, 1))
        radius = jnp.where(low, pltpu.roll(even, 64, 1), odd)
        middle, spread = cm[:, lanes].astype(F32), rm[:, lanes].astype(F32)
        upper = jnp.where(middle > -spread, 0.5 * (center + radius), 0.0)
        lower = jnp.where(middle > spread, 0.5 * (center - radius), 0.0)
        cm_out[:, lanes] = (upper + lower).astype(BF16)
        rm_out[:, lanes] = (upper - lower).astype(BF16)

    def b_wait(k, _):
        ys, half = k // 2, lax.rem(k, 2)
        pltpu.make_async_copy(b_out.at[0], b_in.at[ys, half], b_recv.at[ys, half]).wait()
        return 0

    lax.fori_loop(0, 16, b_wait, 0)
    for half in range(2):
        value = b_in[0, half].astype(F32)
        for ys in range(1, 8):
            value = value + b_in[ys, half].astype(F32)
        value = value * (1.0 / 32.0)
        if half == 0:
            wg_out[0:80, :] = value
        else:
            wg_out[80:144, :] = value[16:80]

    def v_done(k, _):
        v_copy(lax.rem(block + k, 8)).wait_send()
        r_copy(lax.rem(block + k, 8)).wait_send()
        return 0

    lax.fori_loop(1, 8, v_done, 0)

    @pl.when(down)
    def _():
        vh_down.wait_send()
        h_down.wait_send()

    @pl.when(up)
    def _():
        vh_up.wait_send()
        h_up.wait_send()

    def q_done(q, _):
        for k in range(1, 4):
            g_copy(q, lax.rem(x + k, 4)).wait_send()

        @pl.when(w_source)
        def _():
            def to_y(k, _):
                w_copy(q, lax.rem(y + k, 8)).wait_send()
                return 0

            lax.fori_loop(1, 8, to_y, 0)

            @pl.when(c != w_core)
            def _():
                w_copy(q, y).wait_send()

        p_copy(q).wait_send()
        wz_copy(q).wait_send()

        def rs_done(k, _):
            rs_copy(q, lax.rem(z + k, 8)).wait_send()
            return 0

        lax.fori_loop(1, 8, rs_done, 0)
        for k in range(4):
            xf = lax.rem(x + k, 4)

            @pl.when(jnp.logical_not(b_is_self(q, xf)))
            def _():
                b_copy(q, xf).wait_send()
        return 0

    lax.fori_loop(0, 4, q_done, 0)


def on_device(center_mid, radius_mid, conv_weight, center_upstream, radius_upstream):
    flat = [v.reshape(128, 512) for v in (center_mid, radius_mid, center_upstream, radius_upstream)]
    weight = conv_weight.reshape(16, 3, 3, 4, 128).transpose(3, 2, 0, 1, 4).reshape(4, 3, 16, 384)
    dma = pltpu.SemaphoreType.DMA
    hbm, vmem = pl.BlockSpec(memory_space=pl.ANY), pl.BlockSpec(memory_space=pltpu.VMEM)
    center_grad, radius_grad, weight_grad = pl.pallas_call(
        kernel,
        out_shape=(
            jax.ShapeDtypeStruct((128, 512), BF16),
            jax.ShapeDtypeStruct((128, 512), BF16),
            jax.ShapeDtypeStruct((144, 128), F32),
        ),
        in_specs=[hbm, hbm, hbm, hbm, vmem],
        out_specs=(vmem, vmem, vmem),
        scratch_shapes=[
            pltpu.VMEM((128, 512), BF16),
            pltpu.VMEM((128, 512), BF16),
            pltpu.VMEM((8, 128, 128), BF16),
            pltpu.VMEM((2, 576, 128), BF16),
            pltpu.VMEM((2, 192, 1152), BF16),
            pltpu.VMEM((4, 2, 2, 640, 128), BF16),
            pltpu.VMEM((4, 3, 4, 16, 384), BF16),
            pltpu.VMEM((2, 1152, 256), F32),
            pltpu.VMEM((4, 8, 80, 128), BF16),
            pltpu.VMEM((4, 8, 80, 128), BF16),
            pltpu.VMEM((4, 80, 128), BF16),
            pltpu.VMEM((8, 2, 80, 128), BF16),
            pltpu.VMEM((2, 2, 32, 128), F32),
            pltpu.VMEM((2, 2, 32, 128), F32),
            pltpu.VMEM((1152, 128), F32),
            pltpu.VMEM((2, 512, 128), BF16),
            pltpu.VMEM((8, 128, 128), BF16),
            dma((2,)), dma((4, 2)), dma((8,)), dma((8,)), dma((2,)), dma((2,)), dma((4, 4)), dma((4, 4)),
            dma((4,)), dma((4,)), dma((4, 8)), dma((4, 2)), dma((4,)), dma((4,)), dma((4, 8)), dma((4, 8)),
            dma((4, 4)), dma((8, 2)), dma((2,)), dma((2,)), dma((8,)), dma((8,)),
        ],
        compiler_params=pltpu.CompilerParams(
            collective_id=0, has_side_effects=True, vmem_limit_bytes=48 << 20
        ),
    )(flat[0], flat[1], flat[2], flat[3], weight)
    x = lax.rem(lax.axis_index("rows"), 4)
    own = lax.dynamic_slice_in_dim(weight_grad, x * 32, 32, axis=1)
    return (
        center_grad.reshape(center_mid.shape),
        radius_grad.reshape(center_mid.shape),
        own.reshape(3, 3, 16, 32).transpose(2, 0, 1, 3),
    )


def solution(mesh):
    placed = (
        P("img", "rows", None, None),
        P("img", "rows", None, None),
        P("img", None, None, None),
        P("img", "rows", None, None),
        P("img", "rows", None, None),
    )
    return jax.shard_map(
        on_device,
        mesh=mesh,
        in_specs=placed,
        out_specs=(
            P("img", "rows", None, None),
            P("img", "rows", None, None),
            P("img", None, None, "rows"),
        ),
        check_vma=False,
    )
```

time: 325 us -> 121 us (0.37)
  the two profiles are of different devices: /device:TPU:8 before, /device:TPU:113 now
where the time goes in v1:
time: 121 us
  Pallas kernels  116 us (96%)
  local copies, waits for them, and re-layouts  4.1 us (3%)
    pallas_call x1, Pallas kernels, on_device(): pl.pallas_call(kernel, out_shape=(jax.ShapeDtypeStruct((128, 512), BF16),...  116 us

profile of v1, /device:TPU:113, one launch (start us, length us, event | category | flops | bytes accessed | tf_op | source)
XLA Modules:
  0.0 120.7 jit_solution(10904777153950567277)
XLA Ops:
  0.6 0.9 reshape.37
  1.6 0.0 copy-start.2
  1.6 0.0 copy-start.3
  1.6 0.1 copy.11
  1.7 0.0 copy-start
  1.8 0.0 copy-start.1
  1.8 0.1 reshape.38.w_ref
  1.9 0.6 copy-done.2
  2.5 0.1 copy-done.3
  2.6 0.1 copy-done
  2.7 0.1 copy-done.1
  2.7 115.9 %shard_map.76 = (bf16[128,512]{1,0:T(8,128)(2,1)S(1)}, bf16[128,512]{1,0:T(8,128)(2,1)S(1)}, f32[144,128]{1,0:T(8,128)S(1)}) custom-call(bf16[128,512]{1,0:T(8,128)(2,1)S(1)} %bitcast.18, bf16[128,512]{1,0:T(8,128)(2,1)S(1)} %bitcast.19, bf16[128,512]{1,0:T(8,128)(2,1)S(1)} %bitcast.20, bf16[128,512]{1,0:T(8,128)(2,1)S(1)} %bitcast.21, ...), custom_call_target="tpu_custom_call" | custom-call | tf_op jit(solution)/shard_map/pallas_call | solution.py:533
  118.7 0.7 constant_dynamic-slice_fusion
  119.4 0.7 copy.14
  120.1 0.7 copy.15
Async XLA Ops:
  1.6 0.9 copy-start.2
  1.6 1.0 copy-start.3
  1.7 0.9 copy-start
  1.8 1.0 copy-start.1

commit v2 on v1

--- a/solution.py
+++ b/solution.py
@@ -27,9 +27,9 @@
 def kernel(
     cm_hbm, rm_hbm, gc_hbm, gr_hbm, w_ref,
     cm_out, rm_out, wg_out,
-    cm, rm, vsend, vbuf, vt, gbuf, wbuf, acc, rs_out, rs_in, b_out, b_in, halo_out, halo_in, total, r_out, r_in,
+    cm, rm, vsend, vbuf, vt, gbuf, wbuf, acc, rs_out, rs_in, a_out, a_in, c_out, c_in, halo_out, halo_in, total, r_out, r_in,
     load_sem, gload_sem, v_send, v_recv, vh_send, vh_recv, g_send, g_recv, p_send, p_recv,
-    w_send, w_recv, wz_send, wz_recv, rs_send, rs_recv, b_send, b_recv, h_send, h_recv, r_send, r_recv,
+    w_send, w_recv, wz_send, wz_recv, rs_send, rs_recv, a_send, a_recv, c_send, c_recv, h_send, h_recv, r_send, r_recv,
 ):
     i_img, i_rows = lax.axis_index("img"), lax.axis_index("rows")
     x, z_hi = lax.rem(i_rows, 4), i_rows // 4
@@ -72,16 +72,18 @@
         return 0
 
     lax.fori_loop(1, 8, greet_z, 0)
-    for cf in range(2):
-        @pl.when(jnp.logical_or(y != block, c != cf))
-        def _():
-            greet(place(x, block, z, cf))
-
-    b_self = jnp.logical_and(y == block, part_core == c)
-
-    def greet_b(k, _):
-        ys, half = k // 2, lax.rem(k, 2)
-        xs, cs, zs = lax.rem(y, 4), y // 4, 2 * (2 * c + half) + z_lo
+    def greet_y(k, _):
+        greet(place(x, lax.rem(y + k, 8), z, c))
+        return 0
+
+    lax.fori_loop(1, 8, greet_y, 0)
+    greet(place(x, block, z, 1 - c))
+    q_own, u_own = y // 2, lax.rem(y, 2)
+    own_part = (y == block) & (q_own == z_hi) & (part_core == c)
+
+    def greet_owner(k, _):
+        half, u = k // 2, lax.rem(k, 2)
+        xs, ys, zs, cs = lax.rem(y, 4), 2 * z_hi + u, 2 * (2 * c + half) + z_lo, y // 4
         same = (xs == x) & (ys == y) & (zs == z) & (cs == c)
 
         @pl.when(jnp.logical_not(same))
@@ -89,11 +91,9 @@
             greet(place(xs, ys, zs, cs))
         return 0
 
-    lax.fori_loop(0, 16, greet_b, 0)
+    lax.fori_loop(0, 4, greet_owner, 0)
     expected = (
-        30
-        + jnp.where(w_source, 8 - jnp.where(c == w_core, 1, 0), 0)
-        - jnp.where(b_self, 1, 0)
+        25 + jnp.where(w_source & (c != w_core), 8, 0) - jnp.where(own_part, 1, 0)
     )
 
     zero_rows = jnp.zeros((64, 128), BF16)
@@ -285,15 +285,16 @@
             rs_out.at[q, zd], rs_in.at[q, z], rs_send.at[q, zd], rs_recv.at[q, z], place(x, y, zd, c)
         )
 
-    def b_place(q, xf):
-        return place(xf, block, 2 * q + z_lo, part_core)
-
-    def b_is_self(q, xf):
-        return (xf == x) & b_self & (q == z_hi)
-
-    def b_copy(q, xf):
+    def a_copy(q, u):
         return remote(
-            b_out.at[q], b_in.at[y, part_half], b_send.at[q, xf], b_recv.at[y, part_half], b_place(q, xf)
+            a_out.at[q, 32 * u : 32 * u + 48], a_in.at[y], a_send.at[q, u], a_recv.at[y],
+            place(x, 2 * q + u, z, c),
+        )
+
+    def c_copy(xf):
+        return remote(
+            c_out, c_in.at[part_half, u_own], c_send.at[xf], c_recv.at[part_half, u_own],
+            place(xf, block, 2 * q_own + z_lo, part_core),
         )
 
     def reduce_z(q):
@@ -305,19 +306,42 @@
         value = rs_in[q, 0].astype(F32)
         for zs in range(1, 8):
             value = value + rs_in[q, zs].astype(F32)
-        b_out[q] = value.astype(BF16)
+        a_out[q] = value.astype(BF16)
+        for u in range(2):
+            @pl.when(y == 2 * q + u)
+            def _():
+                pltpu.make_async_copy(
+                    a_out.at[q, 32 * u : 32 * u + 48], a_in.at[y], a_recv.at[y]
+                ).start()
+
+            @pl.when(y != 2 * q + u)
+            def _():
+                a_copy(q, u).start()
+
+    def reduce_y():
+        def one(ys, _):
+            pltpu.make_async_copy(a_out.at[0, 0:48], a_in.at[ys], a_recv.at[ys]).wait()
+            return 0
+
+        lax.fori_loop(0, 8, one, 0)
+        value = a_in[0].astype(F32)
+        for ys in range(1, 8):
+            value = value + a_in[ys].astype(F32)
+        c_out[...] = value.astype(BF16)
         for k in range(4):
             xf = lax.rem(x + k, 4)
-
-            @pl.when(b_is_self(q, xf))
-            def _():
-                pltpu.make_async_copy(
-                    b_out.at[q], b_in.at[y, part_half], b_recv.at[y, part_half]
-                ).start()
-
-            @pl.when(jnp.logical_not(b_is_self(q, xf)))
-            def _():
-                b_copy(q, xf).start()
+            if k == 0:
+                @pl.when(own_part)
+                def _():
+                    pltpu.make_async_copy(
+                        c_out, c_in.at[part_half, u_own], c_recv.at[part_half, u_own]
+                    ).start()
+
+                @pl.when(jnp.logical_not(own_part))
+                def _():
+                    c_copy(xf).start()
+            else:
+                c_copy(xf).start()
 
     def step(q, _):
         p_wait(q)
@@ -440,6 +464,8 @@
     for b in (0, 3, 4, 7):
         r_send_to(b)
 
+    reduce_y()
+
     def r_wait(b, _):
         pltpu.make_async_copy(r_out.at[0, 0:128], r_in.at[b], r_recv.at[b]).wait()
         return 0
@@ -457,21 +483,18 @@
         cm_out[:, lanes] = (upper + lower).astype(BF16)
         rm_out[:, lanes] = (upper - lower).astype(BF16)
 
-    def b_wait(k, _):
-        ys, half = k // 2, lax.rem(k, 2)
-        pltpu.make_async_copy(b_out.at[0], b_in.at[ys, half], b_recv.at[ys, half]).wait()
-        return 0
-
-    lax.fori_loop(0, 16, b_wait, 0)
+    def c_wait(k, _):
+        half, u = k // 2, lax.rem(k, 2)
+        pltpu.make_async_copy(c_out, c_in.at[half, u], c_recv.at[half, u]).wait()
+        return 0
+
+    lax.fori_loop(0, 4, c_wait, 0)
     for half in range(2):
-        value = b_in[0, half].astype(F32)
-        for ys in range(1, 8):
-            value = value + b_in[ys, half].astype(F32)
-        value = value * (1.0 / 32.0)
-        if half == 0:
-            wg_out[0:80, :] = value
-        else:
-            wg_out[80:144, :] = value[16:80]
+        for u in range(2):
+            first = 0 if half == u == 0 else 1
+            wg_out[64 * half + 32 * u + 16 * first : 64 * half + 32 * u + 48, :] = (
+                c_in[half, u, 16 * first : 48, :].astype(F32) * (1.0 / 32.0)
+            )
 
     def v_done(k, _):
         v_copy(lax.rem(block + k, 8)).wait_send()
@@ -514,15 +537,20 @@
             return 0
 
         lax.fori_loop(1, 8, rs_done, 0)
-        for k in range(4):
-            xf = lax.rem(x + k, 4)
-
-            @pl.when(jnp.logical_not(b_is_self(q, xf)))
+        for u in range(2):
+            @pl.when(y != 2 * q + u)
             def _():
-                b_copy(q, xf).wait_send()
+                a_copy(q, u).wait_send()
         return 0
 
     lax.fori_loop(0, 4, q_done, 0)
+    for k in range(4):
+        if k == 0:
+            @pl.when(jnp.logical_not(own_part))
+            def _():
+                c_copy(x).wait_send()
+        else:
+            c_copy(lax.rem(x + k, 4)).wait_send()
 
 
 def on_device(center_mid, radius_mid, conv_weight, center_upstream, radius_upstream):
@@ -551,7 +579,9 @@
             pltpu.VMEM((4, 8, 80, 128), BF16),
             pltpu.VMEM((4, 8, 80, 128), BF16),
             pltpu.VMEM((4, 80, 128), BF16),
-            pltpu.VMEM((8, 2, 80, 128), BF16),
+            pltpu.VMEM((8, 48, 128), BF16),
+            pltpu.VMEM((48, 128), BF16),
+            pltpu.VMEM((2, 2, 48, 128), BF16),
             pltpu.VMEM((2, 2, 32, 128), F32),
             pltpu.VMEM((2, 2, 32, 128), F32),
             pltpu.VMEM((1152, 128), F32),
@@ -559,7 +589,7 @@
             pltpu.VMEM((8, 128, 128), BF16),
             dma((2,)), dma((4, 2)), dma((8,)), dma((8,)), dma((2,)), dma((2,)), dma((4, 4)), dma((4, 4)),
             dma((4,)), dma((4,)), dma((4, 8)), dma((4, 2)), dma((4,)), dma((4,)), dma((4, 8)), dma((4, 8)),
-            dma((4, 4)), dma((8, 2)), dma((2,)), dma((2,)), dma((8,)), dma((8,)),
+            dma((4, 2)), dma((8,)), dma((4,)), dma((2, 2)), dma((2,)), dma((2,)), dma((8,)), dma((8,)),
         ],
         compiler_params=pltpu.CompilerParams(
             collective_id=0, has_side_effects=True, vmem_limit_bytes=48 << 20

time: 121 us -> 68.8 us (0.57)
  the two profiles are of different devices: /device:TPU:113 before, /device:TPU:57 now
where the time goes in v2:
time: 68.8 us; the launch traced here: 68.6 us
  Pallas kernels  63.8 us (93%)
  local copies, waits for them, and re-layouts  4.1 us (6%)
  between operations  0.7 us (1%)
    pallas_call x1, Pallas kernels, on_device(): pl.pallas_call(kernel, out_shape=(jax.ShapeDtypeStruct((128, 512), BF16),...  63.8 us
    unnamed x10, local copies, waits for them, and re-layouts  2.17 us

profile of v2, /device:TPU:57, one launch (start us, length us, event | category | flops | bytes accessed | tf_op | source)
XLA Modules:
  0.0 68.6 jit_solution(7165314275293029309)
XLA Ops:
  0.6 0.9 %reshape.37 = bf16[16,3,3,4,128]{4,3,0,2,1:T(4,128)(2,1)S(1)} reshape(bf16[16,3,3,512]{3,0,2,1:T(8,128)(2,1)} %param.7) | data formatting | bytes 294912 | tf_op jit(solution)/shard_map/reshape | solution.py:558
  1.6 0.0 copy-start.2
  1.6 0.0 copy-start.3
  1.6 0.1 copy.11
  1.7 0.0 copy-start
  1.8 0.0 copy-start.1
  1.8 0.1 reshape.38.w_ref
  1.9 0.6 copy-done.2
  2.5 0.1 copy-done.3
  2.6 0.1 copy-done
  2.7 0.1 copy-done.1
  2.7 63.8 %shard_map.76 = (bf16[128,512]{1,0:T(8,128)(2,1)S(1)}, bf16[128,512]{1,0:T(8,128)(2,1)S(1)}, f32[144,128]{1,0:T(8,128)S(1)}) custom-call(bf16[128,512]{1,0:T(8,128)(2,1)S(1)} %bitcast.18, bf16[128,512]{1,0:T(8,128)(2,1)S(1)} %bitcast.19, bf16[128,512]{1,0:T(8,128)(2,1)S(1)} %bitcast.20, bf16[128,512]{1,0:T(8,128)(2,1)S(1)} %bitcast.21, ...), custom_call_target="tpu_custom_call" | custom-call | tf_op jit(solution)/shard_map/pallas_call | solution.py:561
  66.6 0.7 %constant_dynamic-slice_fusion = f32[144,32]{1,0:T(8,128)} fusion(f32[144,128]{1,0:T(8,128)S(1)} %get-tuple-element.8, s32[]{:T(128)S(6)} %select_n.3), kind=kLoop, calls=%fused_computation.1 | loop fusion | bytes 36868 | tf_op jit(solution)/shard_map/dynamic_slice | solution.py:599
  67.3 0.7 copy.14
  68.0 0.7 copy.15
Async XLA Ops:
  1.6 0.9 %copy-start.2 = (bf16[1,4,32,512]{3,2,1,0:T(8,128)(2,1)S(1)}, bf16[1,4,32,512]{3,2,1,0:T(8,128)(2,1)}, u32[]{:S(2)}) copy-start(bf16[1,4,32,512]{3,2,1,0:T(8,128)(2,1)} %param.8) | copy-start | bytes 393220
  1.6 1.0 %copy-start.3 = (bf16[1,4,32,512]{3,2,1,0:T(8,128)(2,1)S(1)}, bf16[1,4,32,512]{3,2,1,0:T(8,128)(2,1)}, u32[]{:S(2)}) copy-start(bf16[1,4,32,512]{3,2,1,0:T(8,128)(2,1)} %param.9) | copy-start | bytes 393220
  1.7 0.9 %copy-start = (bf16[1,4,32,512]{3,2,1,0:T(8,128)(2,1)S(1)}, bf16[1,4,32,512]{3,2,1,0:T(8,128)(2,1)}, u32[]{:S(2)}) copy-start(bf16[1,4,32,512]{3,2,1,0:T(8,128)(2,1)} %param.5) | copy-start | bytes 393220
  1.8 1.0 %copy-start.1 = (bf16[1,4,32,512]{3,2,1,0:T(8,128)(2,1)S(1)}, bf16[1,4,32,512]{3,2,1,0:T(8,128)(2,1)}, u32[]{:S(2)}) copy-start(bf16[1,4,32,512]{3,2,1,0:T(8,128)(2,1)} %param.6) | copy-start | bytes 393220

commit v3 on v0

v3 whole, which is shorter than its diff:
```python
import jax
import jax.numpy as jnp
from jax import lax
from jax.experimental import pallas as pl
from jax.experimental.pallas import tpu as pltpu
from jax.sharding import PartitionSpec as P

MESH = pl.DeviceIdType.MESH
F32 = jnp.float32
BF16 = jnp.bfloat16
NQ = 4
LANES = 512 // NQ
QB = 4 // NQ


def rem(value, by):
    return lax.rem(value, jnp.int32(by))


def div(value, by):
    return lax.div(value, jnp.int32(by))


def place(x, y, z, c):
    return ((y * 2 + rem(z, 2)) * 2 + c, div(z, 2) * 4 + x)


def remote(src, dst, send, recv, where):
    return pltpu.make_async_remote_copy(
        src_ref=src, dst_ref=dst, send_sem=send, recv_sem=recv, device_id=where, device_id_type=MESH
    )


def local(src, dst, sem):
    return pltpu.make_async_copy(src, dst, sem)


def bytes_of(ref, sem):
    pltpu.make_async_copy(ref, ref, sem).wait()


def mul(value, by):
    return pl.multiple_of(value, by)


def kernel(
    cm_hbm, rm_hbm, gc_hbm, gr_hbm, w_ref,
    cm_out, rm_out, wg_out,
    cm, rm, vsend, vmain, vhalo, vt, gbuf, wbuf, acc, rs_out, rs_in, a_out, a_in, c_out, c_in,
    halo_out, halo_in, total, r_out, r_in,
    load_sem, gload_sem, v_send, v_recv, vh_send, vh_recv, g_send, g_recv, p_send, p_recv,
    w_send, w_recv, wz_send, wz_recv, rs_send, rs_recv, a_send, a_recv, c_send, c_recv,
    h_send, h_recv, r_send, r_recv,
):
    i_img, i_rows = lax.axis_index("img"), lax.axis_index("rows")
    x, z_hi = rem(i_rows, 4), div(i_rows, 4)
    y, z_lo, c = div(i_img, 4), rem(div(i_img, 2), 2), rem(i_img, 2)
    z = z_hi * 2 + z_lo
    block = x + 4 * c
    w_source = rem(y, 4) == x
    w_core = div(y, 4)
    part_core, part_half = div(z, 4), rem(div(z, 2), 2)
    q_own, u_own = div(y, 2), rem(y, 2)
    own_part = (y == block) & (q_own == z_hi) & (part_core == c)

    barrier = pltpu.get_barrier_semaphore()

    def greet(where):
        pl.semaphore_signal(barrier, inc=1, device_id=where, device_id_type=MESH)

    for k in range(1, 8):
        greet(place(rem(x + k, 4), y, z, rem(c + k // 4, 2)))
        greet(place(x, y, rem(z + k, 8), c))
        greet(place(x, rem(y + k, 8), z, c))
    greet(place(x, block, z, 1 - c))
    for half in range(2):
        for u in range(2):
            xs, ys, zs, cs = rem(y, 4), 2 * z_hi + u, 2 * (2 * c + half) + z_lo, div(y, 4)
            same = (xs == x) & (ys == y) & (zs == z) & (cs == c)

            @pl.when(jnp.logical_not(same))
            def _():
                greet(place(xs, ys, zs, cs))

    expected = 25 + jnp.where(w_source & (c != w_core), 8, 0) - jnp.where(own_part, 1, 0)

    load_cm = local(cm_hbm, cm, load_sem.at[0])
    load_rm = local(rm_hbm, rm, load_sem.at[1])
    load_cm.start()
    load_rm.start()
    own_rows = pl.ds(mul(64 + 128 * x, 64), 128)
    for q in range(NQ):
        for arr, ref in ((0, gc_hbm), (1, gr_hbm)):
            local(
                ref.at[:, LANES * q : LANES * q + LANES], gbuf.at[q, arr, c, own_rows], gload_sem.at[q]
            ).start()

    load_cm.wait()
    load_rm.wait()
    lane = lax.broadcasted_iota(jnp.int32, (128, 128), 1)
    low = lane < 64
    for j in range(4):
        middle = cm[:, 128 * j : 128 * j + 128].astype(F32)
        spread = rm[:, 128 * j : 128 * j + 128].astype(F32)
        upper = jnp.maximum(middle + spread, 0.0)
        lower = jnp.maximum(middle - spread, 0.0)
        center = (upper + lower) * 0.5
        radius = (upper - lower) * 0.5
        vsend[2 * j] = jnp.where(low, center, pltpu.roll(radius, 64, 1)).astype(BF16)
        vsend[2 * j + 1] = jnp.where(low, pltpu.roll(center, 64, 1), radius).astype(BF16)

    pl.semaphore_wait(barrier, expected)

    v_place = vmain.at[c, pl.ds(mul(128 * x, 128), 128)]
    for k in range(1, 8):
        xd, cd = rem(x + k, 4), rem(c + k // 4, 2)
        remote(vsend.at[xd + 4 * cd], v_place, v_send, v_recv, place(xd, y, z, cd)).start()
    local(vsend.at[block], v_place, v_recv).start()

    own_shard = z_lo * 2 + c

    def start_w(q):
        @pl.when(w_source)
        def _():
            for k in range(1, 8):
                remote(
                    w_ref.at[q], wbuf.at[q, :, own_shard], w_send, w_recv.at[q],
                    place(x, rem(y + k, 8), z, w_core),
                ).start()

            @pl.when(c == w_core)
            def _():
                local(w_ref.at[q], wbuf.at[q, :, own_shard], w_recv.at[q]).start()

            @pl.when(c != w_core)
            def _():
                remote(
                    w_ref.at[q], wbuf.at[q, :, own_shard], w_send, w_recv.at[q], place(x, y, z, w_core)
                ).start()

    def start_g(q):
        own = gbuf.at[q, :, c, own_rows]
        bytes_of(own, gload_sem.at[q])
        for k in range(1, 4):
            remote(own, own, g_send, g_recv.at[q], place(rem(x + k, 4), y, z, c)).start()

    for q in range(NQ):
        start_w(q)
        start_g(q)

    zero_rows = jnp.zeros((64, LANES), BF16)

    def clear(q, _):
        for arr in range(2):
            for image in range(2):
                gbuf[q, arr, image, 0:64, :] = zero_rows
                gbuf[q, arr, image, 576:640, :] = zero_rows
        return 0

    lax.fori_loop(0, NQ, clear, 0)
    for arr in range(2):
        acc[arr] = jnp.zeros((1152, 256), F32)

    bytes_of(vmain, v_recv)
    down, up = z_hi > 0, z_hi < 3
    at_down, at_up = place(x, y, rem(z + 6, 8), c), place(x, y, rem(z + 2, 8), c)
    vh_down = remote(vmain.at[:, 0:32], vhalo.at[:, 1], vh_send.at[0], vh_recv.at[0], at_down)
    vh_up = remote(vmain.at[:, 480:512], vhalo.at[:, 0], vh_send.at[1], vh_recv.at[1], at_up)

    @pl.when(down)
    def _():
        vh_down.start()

    @pl.when(up)
    def _():
        vh_up.start()

    column = lax.broadcasted_iota(jnp.int32, (128, 128), 0) & 31

    def turn(v, piece):
        taps = (
            jnp.where(column == 0, 0.0, pltpu.roll(v, 1, 0)),
            v,
            jnp.where(column == 31, 0.0, pltpu.roll(v, 127, 0)),
        )
        for tap in range(3):
            turned = taps[tap].T.astype(BF16)
            for arr in range(2):
                vt[arr, tap * 64 : tap * 64 + 64, 128 * piece : 128 * piece + 128] = turned[
                    arr * 64 : arr * 64 + 64
                ]

    for piece in range(8):
        turn(vmain[piece // 4, 128 * (piece % 4) : 128 * (piece % 4) + 128, :].astype(F32), piece)

    ahead = rem(z_lo + c, 2) == 0
    at_mate = place(x, y, rem(jnp.where(ahead, z + 1, z + 7), 8), c)
    at_twin = place(x, y, z, 1 - c)

    def forward(q):
        bytes_of(gbuf.at[q, :, c, 64:448], g_recv.at[q])
        ring_rows = gbuf.at[q, :, c, 64:576]
        remote(ring_rows, ring_rows, p_send, p_recv.at[q], at_twin).start()
        shards = wbuf.at[q, :, pl.ds(z_lo * 2, 2)]
        bytes_of(shards, w_recv.at[q])
        remote(shards, shards, wz_send, wz_recv.at[q], at_mate).start()

    forward(0)

    @pl.when(down)
    def _():
        vh_up.wait_recv()

    @pl.when(up)
    def _():
        vh_down.wait_recv()

    @pl.when(jnp.logical_not(down))
    def _():
        vhalo[:, 0] = jnp.zeros((2, 32, 128), BF16)

    @pl.when(jnp.logical_not(up))
    def _():
        vhalo[:, 1] = jnp.zeros((2, 32, 128), BF16)

    turn(vhalo[...].astype(F32).reshape(128, 128), 8)

    def reduce_z(q):
        bytes_of(rs_in.at[q], rs_recv.at[q])
        for qb in range(QB):
            rows = slice(80 * qb, 80 * qb + 80)
            value = rs_in[q, 0, rows].astype(F32)
            for zs in range(1, 8):
                value = value + rs_in[q, zs, rows].astype(F32)
            a_out[q, qb] = value.astype(BF16)
            for u in range(2):
                piece = a_out.at[q, qb, 32 * u : 32 * u + 48]
                to = 2 * (q * QB + qb) + u

                @pl.when(y == to)
                def _():
                    local(piece, a_in.at[y], a_recv).start()

                @pl.when(y != to)
                def _():
                    remote(piece, a_in.at[y], a_send, a_recv, place(x, to, z, c)).start()

    def step(q, _):
        @pl.when(q < NQ - 1)
        def _():
            forward(q + 1)

        bytes_of(gbuf.at[q, :, 1 - c, 64:576], p_recv.at[q])
        bytes_of(wbuf.at[q, :, pl.ds((1 - z_lo) * 2, 2)], wz_recv.at[q])
        kern = wbuf[q].reshape(192, 3 * LANES)
        windows = []
        for arr in range(2):
            views = []
            for image in range(2):
                views.append(
                    jnp.concatenate(
                        [gbuf[q, arr, image, 96 - 32 * a : 608 - 32 * a, :] for a in range(3)], axis=1
                    )
                )
            for image in range(2):
                for first in (64, 608):
                    views.append(
                        jnp.concatenate(
                            [gbuf[q, arr, image, first - 32 * a : first + 32 - 32 * a, :] for a in range(3)],
                            axis=1,
                        )
                    )
            windows.append(jnp.concatenate(views, axis=0))
        terms = [jnp.dot(vt[arr], windows[arr], preferred_element_type=F32) for arr in range(2)]
        wide = kern.astype(F32)
        signed = jnp.where(wide > 0, terms[1], jnp.where(wide < 0, -terms[1], 0.0))
        partial = (terms[0] + signed).astype(BF16)
        for zd in range(8):
            shard, half = (zd % 2) * 2 + zd // 4, (zd // 2) % 2
            for qb in range(QB):
                for k in range(5):
                    a, tap = divmod(4 * half + k, 3)
                    rs_out[q, zd, 80 * qb + 16 * k : 80 * qb + 16 * k + 16, :] = partial[
                        tap * 64 + shard * 16 : tap * 64 + shard * 16 + 16,
                        a * LANES + 128 * qb : a * LANES + 128 * qb + 128,
                    ]
        local(rs_out.at[q, z], rs_in.at[q, z], rs_recv.at[q]).start()
        for k in range(1, 8):
            zd = rem(z + k, 8)
            remote(rs_out.at[q, zd], rs_in.at[q, z], rs_send, rs_recv.at[q], place(x, y, zd, c)).start()
        for arr, factor in ((0, kern), (1, jnp.abs(kern))):
            acc[arr, :, 0:192] += lax.dot_general(
                windows[arr], factor, (((1,), (1,)), ((), ())), preferred_element_type=F32
            )

        @pl.when(q > 0)
        def _():
            reduce_z(q - 1)
        return 0

    lax.fori_loop(0, NQ, step, 0)

    column64 = lax.broadcasted_iota(jnp.int32, (64, 128), 0) & 31
    low64 = lax.broadcasted_iota(jnp.int32, (64, 128), 1) < 64

    def fold(k, _):
        rows = pl.ds(mul(k * 64, 64), 64)
        c01, r01 = acc[0, rows, 0:128], acc[1, rows, 0:128]
        c2, r2 = acc[0, rows, 128:256], acc[1, rows, 128:256]
        first = jnp.where(low64, c01, pltpu.roll(r01, 64, 1))
        middle = jnp.where(low64, pltpu.roll(c01, 64, 1), r01)
        last = jnp.where(low64, c2, pltpu.roll(r2, 64, 1))
        value = (
            middle
            + jnp.where(column64 == 31, 0.0, pltpu.roll(first, 63, 0))
            + jnp.where(column64 == 0, 0.0, pltpu.roll(last, 1, 0))
        )
        total[rows, :] = value
        return 0

    lax.fori_loop(16, 18, fold, 0)
    for image in range(2):
        for side in range(2):
            first = 1024 + 64 * image + 32 * side
            halo_out[side, image] = total[first : first + 32, :]
    h_down = remote(halo_out.at[0], halo_in.at[0], h_send.at[0], h_recv.at[0], at_down)
    h_up = remote(halo_out.at[1], halo_in.at[1], h_send.at[1], h_recv.at[1], at_up)

    @pl.when(down)
    def _():
        h_down.start()

    @pl.when(up)
    def _():
        h_up.start()

    lax.fori_loop(0, 16, fold, 0)
    for image in range(2):
        r_out[image] = total[512 * image : 512 * image + 512, :].astype(BF16)

    def r_start(b):
        @pl.when(b == block)
        def _():
            local(r_out.at[c, pl.ds(mul(128 * x, 128), 128)], r_in.at[block], r_recv).start()

        @pl.when(b != block)
        def _():
            remote(
                r_out.at[b // 4, 128 * (b % 4) : 128 * (b % 4) + 128], r_in.at[block], r_send, r_recv,
                place(b % 4, y, z, b // 4),
            ).start()

    for b in (1, 2, 5, 6):
        r_start(b)
    reduce_z(NQ - 1)

    @pl.when(up)
    def _():
        h_down.wait_recv()
        for image in range(2):
            r_out[image, 480:512, :] = (total[512 * image + 480 : 512 * image + 512, :] + halo_in[0, image]).astype(BF16)

    @pl.when(down)
    def _():
        h_up.wait_recv()
        for image in range(2):
            r_out[image, 0:32, :] = (total[512 * image : 512 * image + 32, :] + halo_in[1, image]).astype(BF16)

    for b in (0, 3, 4, 7):
        r_start(b)

    bytes_of(a_in, a_recv)
    value = a_in[0].astype(F32)
    for ys in range(1, 8):
        value = value + a_in[ys].astype(F32)
    c_out[...] = value.astype(BF16)
    slot = c_in.at[2 * part_half + u_own]

    @pl.when(own_part)
    def _():
        local(c_out, slot, c_recv).start()

    @pl.when(jnp.logical_not(own_part))
    def _():
        remote(c_out, slot, c_send, c_recv, place(x, block, 2 * q_own + z_lo, part_core)).start()

    for k in range(1, 4):
        remote(
            c_out, slot, c_send, c_recv, place(rem(x + k, 4), block, 2 * q_own + z_lo, part_core)
        ).start()

    bytes_of(r_in, r_recv)
    for j in range(4):
        lanes = slice(128 * j, 128 * j + 128)
        even, odd = r_in[2 * j].astype(F32), r_in[2 * j + 1].astype(F32)
        center = jnp.where(low, even, pltpu.roll(odd, 64, 1))
        radius = jnp.where(low, pltpu.roll(even, 64, 1), odd)
        middle, spread = cm[:, lanes].astype(F32), rm[:, lanes].astype(F32)
        upper = jnp.where(middle > -spread, 0.5 * (center + radius), 0.0)
        lower = jnp.where(middle > spread, 0.5 * (center - radius), 0.0)
        cm_out[:, lanes] = (upper + lower).astype(BF16)
        rm_out[:, lanes] = (upper - lower).astype(BF16)

    bytes_of(vsend.at[0:7], v_send)
    bytes_of(r_in.at[0:7], r_send)

    @pl.when(down)
    def _():
        vh_down.wait_send()
        h_down.wait_send()

    @pl.when(up)
    def _():
        vh_up.wait_send()
        h_up.wait_send()

    bytes_of(gbuf.at[:, :, c, 64:448], g_send)
    bytes_of(gbuf.at[:, :, c, 64:576], p_send)
    bytes_of(wbuf.at[:, :, pl.ds(z_lo * 2, 2)], wz_send)

    @pl.when(w_source & (c == w_core))
    def _():
        bytes_of(acc.at[0, 0:1008], w_send)

    @pl.when(w_source & (c != w_core))
    def _():
        bytes_of(acc.at[0], w_send)

    bytes_of(rs_out.at[:, 0:7], rs_send)
    bytes_of(a_in.at[0:7], a_send)

    @pl.when(own_part)
    def _():
        bytes_of(c_in.at[0:3], c_send)

    @pl.when(jnp.logical_not(own_part))
    def _():
        bytes_of(c_in, c_send)

    bytes_of(c_in, c_recv)
    for half in range(2):
        for u in range(2):
            first = 0 if half == u == 0 else 1
            wg_out[64 * half + 32 * u + 16 * first : 64 * half + 32 * u + 48, :] = (
                c_in[2 * half + u, 16 * first : 48, :].astype(F32) * (1.0 / 32.0)
            )


def on_device(center_mid, radius_mid, conv_weight, center_upstream, radius_upstream):
    flat = [v.reshape(128, 512) for v in (center_mid, radius_mid, center_upstream, radius_upstream)]
    weight = conv_weight.reshape(16, 3, 3, NQ, LANES).transpose(3, 2, 0, 1, 4)
    weight = weight.reshape(NQ, 3, 16, 3 * LANES)
    dma = pltpu.SemaphoreType.DMA
    hbm, vmem = pl.BlockSpec(memory_space=pl.ANY), pl.BlockSpec(memory_space=pltpu.VMEM)
    center_grad, radius_grad, weight_grad = pl.pallas_call(
        kernel,
        out_shape=(
            jax.ShapeDtypeStruct((128, 512), BF16),
            jax.ShapeDtypeStruct((128, 512), BF16),
            jax.ShapeDtypeStruct((144, 128), F32),
        ),
        in_specs=[hbm, hbm, hbm, hbm, vmem],
        out_specs=(vmem, vmem, vmem),
        scratch_shapes=[
            pltpu.VMEM((128, 512), BF16),
            pltpu.VMEM((128, 512), BF16),
            pltpu.VMEM((8, 128, 128), BF16),
            pltpu.VMEM((2, 512, 128), BF16),
            pltpu.VMEM((2, 2, 32, 128), BF16),
            pltpu.VMEM((2, 192, 1152), BF16),
            pltpu.VMEM((NQ, 2, 2, 640, LANES), BF16),
            pltpu.VMEM((NQ, 3, 4, 16, 3 * LANES), BF16),
            pltpu.VMEM((2, 1152, 256), F32),
            pltpu.VMEM((NQ, 8, 80 * QB, 128), BF16),
            pltpu.VMEM((NQ, 8, 80 * QB, 128), BF16),
            pltpu.VMEM((NQ, QB, 80, 128), BF16),
            pltpu.VMEM((8, 48, 128), BF16),
            pltpu.VMEM((48, 128), BF16),
            pltpu.VMEM((4, 48, 128), BF16),
            pltpu.VMEM((2, 2, 32, 128), F32),
            pltpu.VMEM((2, 2, 32, 128), F32),
            pltpu.VMEM((1152, 128), F32),
            pltpu.VMEM((2, 512, 128), BF16),
            pltpu.VMEM((8, 128, 128), BF16),
            dma((2,)), dma((NQ,)), dma, dma, dma((2,)), dma((2,)), dma, dma((NQ,)), dma, dma((NQ,)),
            dma, dma((NQ,)), dma, dma((NQ,)), dma, dma((NQ,)), dma, dma, dma, dma,
            dma((2,)), dma((2,)), dma, dma,
        ],
        compiler_params=pltpu.CompilerParams(
            collective_id=0, has_side_effects=True, vmem_limit_bytes=48 << 20
        ),
    )(flat[0], flat[1], flat[2], flat[3], weight)
    x = lax.rem(lax.axis_index("rows"), 4)
    own = lax.dynamic_slice_in_dim(weight_grad, x * 32, 32, axis=1)
    return (
        center_grad.reshape(center_mid.shape),
        radius_grad.reshape(center_mid.shape),
        own.reshape(3, 3, 16, 32).transpose(2, 0, 1, 3),
    )


def solution(mesh):
    placed = (
        P("img", "rows", None, None),
        P("img", "rows", None, None),
        P("img", None, None, None),
        P("img", "rows", None, None),
        P("img", "rows", None, None),
    )
    return jax.shard_map(
        on_device,
        mesh=mesh,
        in_specs=placed,
        out_specs=(
            P("img", "rows", None, None),
            P("img", "rows", None, None),
            P("img", None, None, "rows"),
        ),
        check_vma=False,
    )
```

time: 325 us -> 61.4 us (0.19)
  the two profiles are of different devices: /device:TPU:8 before, /device:TPU:7 now
where the time goes in v3:
time: 61.4 us; the launch traced here: 61.2 us
  Pallas kernels  56.4 us (92%)
  local copies, waits for them, and re-layouts  4.1 us (7%)
  between operations  0.7 us (1%)
    pallas_call x1, Pallas kernels, on_device(): pl.pallas_call(kernel, out_shape=(jax.ShapeDtypeStruct((128, 512), BF16),...  56.4 us
    unnamed x10, local copies, waits for them, and re-layouts  2.17 us

profile of v3, /device:TPU:7, one launch (start us, length us, event | category | flops | bytes accessed | tf_op | source)
XLA Modules:
  0.0 61.2 jit_solution(13814673436588863180)
XLA Ops:
  0.6 0.9 %reshape.37 = bf16[16,3,3,4,128]{4,3,0,2,1:T(4,128)(2,1)S(1)} reshape(bf16[16,3,3,512]{3,0,2,1:T(8,128)(2,1)} %param.7) | data formatting | bytes 294912 | tf_op jit(solution)/shard_map/reshape | solution.py:451
  1.6 0.0 copy-start.2
  1.6 0.0 copy-start.3
  1.6 0.1 copy.11
  1.7 0.0 copy-start
  1.8 0.0 copy-start.1
  1.8 0.1 reshape.38.w_ref
  1.9 0.6 copy-done.2
  2.5 0.1 copy-done.3
  2.6 0.1 copy-done
  2.7 0.1 copy-done.1
  2.7 56.4 %shard_map.76 = (bf16[128,512]{1,0:T(8,128)(2,1)S(1)}, bf16[128,512]{1,0:T(8,128)(2,1)S(1)}, f32[144,128]{1,0:T(8,128)S(1)}) custom-call(bf16[128,512]{1,0:T(8,128)(2,1)S(1)} %bitcast.18, bf16[128,512]{1,0:T(8,128)(2,1)S(1)} %bitcast.19, bf16[128,512]{1,0:T(8,128)(2,1)S(1)} %bitcast.20, bf16[128,512]{1,0:T(8,128)(2,1)S(1)} %bitcast.21, ...), custom_call_target="tpu_custom_call" | custom-call | tf_op jit(solution)/shard_map/pallas_call | solution.py:455
  59.2 0.7 %constant_dynamic-slice_fusion = f32[144,32]{1,0:T(8,128)} fusion(f32[144,128]{1,0:T(8,128)S(1)} %get-tuple-element.8, s32[]{:T(128)S(6)} %select_n.3), kind=kLoop, calls=%fused_computation.1 | loop fusion | bytes 36868 | tf_op jit(solution)/shard_map/dynamic_slice | solution.py:494
  59.9 0.7 %copy.14 = bf16[1,4,32,512]{3,2,1,0:T(8,128)(2,1)} copy(bf16[1,4,32,512]{3,2,1,0:T(8,128)(2,1)S(1)} %bitcast.17) | data formatting | bytes 262144
  60.6 0.7 %copy.15 = bf16[1,4,32,512]{3,2,1,0:T(8,128)(2,1)} copy(bf16[1,4,32,512]{3,2,1,0:T(8,128)(2,1)S(1)} %bitcast.16) | data formatting | bytes 262144
Async XLA Ops:
  1.6 0.9 %copy-start.2 = (bf16[1,4,32,512]{3,2,1,0:T(8,128)(2,1)S(1)}, bf16[1,4,32,512]{3,2,1,0:T(8,128)(2,1)}, u32[]{:S(2)}) copy-start(bf16[1,4,32,512]{3,2,1,0:T(8,128)(2,1)} %param.8) | copy-start | bytes 393220
  1.6 1.0 %copy-start.3 = (bf16[1,4,32,512]{3,2,1,0:T(8,128)(2,1)S(1)}, bf16[1,4,32,512]{3,2,1,0:T(8,128)(2,1)}, u32[]{:S(2)}) copy-start(bf16[1,4,32,512]{3,2,1,0:T(8,128)(2,1)} %param.9) | copy-start | bytes 393220
  1.7 0.9 %copy-start = (bf16[1,4,32,512]{3,2,1,0:T(8,128)(2,1)S(1)}, bf16[1,4,32,512]{3,2,1,0:T(8,128)(2,1)}, u32[]{:S(2)}) copy-start(bf16[1,4,32,512]{3,2,1,0:T(8,128)(2,1)} %param.5) | copy-start | bytes 393220
  1.8 1.0 %copy-start.1 = (bf16[1,4,32,512]{3,2,1,0:T(8,128)(2,1)S(1)}, bf16[1,4,32,512]{3,2,1,0:T(8,128)(2,1)}, u32[]{:S(2)}) copy-start(bf16[1,4,32,512]{3,2,1,0:T(8,128)(2,1)} %param.6) | copy-start | bytes 393220

commit v4 on v3

--- a/solution.py
+++ b/solution.py
@@ -46,10 +46,10 @@
 def kernel(
     cm_hbm, rm_hbm, gc_hbm, gr_hbm, w_ref,
     cm_out, rm_out, wg_out,
-    cm, rm, vsend, vmain, vhalo, vt, gbuf, wbuf, acc, rs_out, rs_in, a_out, a_in, c_out, c_in,
+    cm, rm, vsend, vmain, vhalo, vt, gbuf, wbuf, acc, rs_out, rs_in, ry_out, ry_in, a_out, a_in, ay_out, ay_in, c_out, c_in, cy_out, cy_in,
     halo_out, halo_in, total, r_out, r_in,
     load_sem, gload_sem, v_send, v_recv, vh_send, vh_recv, g_send, g_recv, p_send, p_recv,
-    w_send, w_recv, wz_send, wz_recv, rs_send, rs_recv, a_send, a_recv, c_send, c_recv,
+    w_send, w_recv, wz_send, wz_recv, rs_send, rs_recv, ry_send, ry_recv, a_send, a_recv, ay_send, ay_recv, c_send, c_recv, cy_send, cy_recv,
     h_send, h_recv, r_send, r_recv,
 ):
     i_img, i_rows = lax.axis_index("img"), lax.axis_index("rows")
@@ -60,8 +60,11 @@
     w_source = rem(y, 4) == x
     w_core = div(y, 4)
     part_core, part_half = div(z, 4), rem(div(z, 2), 2)
-    q_own, u_own = div(y, 2), rem(y, 2)
-    own_part = (y == block) & (q_own == z_hi) & (part_core == c)
+    sums_y = y == block
+    part_own = part_core == c
+    sums_z = z_lo == div(y, 4)
+    core_y, half_y = rem(div(y, 2), 2), rem(y, 2)
+    own_y = (y == block) & (core_y == c)
 
     barrier = pltpu.get_barrier_semaphore()
 
@@ -74,15 +77,26 @@
         greet(place(x, rem(y + k, 8), z, c))
     greet(place(x, block, z, 1 - c))
     for half in range(2):
-        for u in range(2):
-            xs, ys, zs, cs = rem(y, 4), 2 * z_hi + u, 2 * (2 * c + half) + z_lo, div(y, 4)
-            same = (xs == x) & (ys == y) & (zs == z) & (cs == c)
-
-            @pl.when(jnp.logical_not(same))
-            def _():
-                greet(place(xs, ys, zs, cs))
-
-    expected = 25 + jnp.where(w_source & (c != w_core), 8, 0) - jnp.where(own_part, 1, 0)
+        xs, zs, cs = rem(y, 4), 2 * (2 * c + half) + z_lo, div(y, 4)
+        same = (xs == x) & (zs == z) & (cs == c)
+
+        @pl.when(jnp.logical_not(same))
+        def _():
+            greet(place(xs, y, zs, cs))
+
+        ys = 4 * z_lo + 2 * c + half
+        same_y = (xs == x) & (ys == y) & (cs == c)
+
+        @pl.when(jnp.logical_not(same_y))
+        def _():
+            greet(place(xs, ys, z, cs))
+
+    expected = (
+        21
+        + jnp.where(sums_z, 4 - jnp.where(own_y, 1, 0), 0)
+        + jnp.where(w_source & (c != w_core), 8, 0)
+        + jnp.where(sums_y, 16 - jnp.where(part_own, 1, 0), 0)
+    )
 
     load_cm = local(cm_hbm, cm, load_sem.at[0])
     load_rm = local(rm_hbm, rm, load_sem.at[1])
@@ -197,16 +211,21 @@
     at_mate = place(x, y, rem(jnp.where(ahead, z + 1, z + 7), 8), c)
     at_twin = place(x, y, z, 1 - c)
 
-    def forward(q):
+    def forward_g(q):
         bytes_of(gbuf.at[q, :, c, 64:448], g_recv.at[q])
         ring_rows = gbuf.at[q, :, c, 64:576]
         remote(ring_rows, ring_rows, p_send, p_recv.at[q], at_twin).start()
+
+    def forward_w(q):
         shards = wbuf.at[q, :, pl.ds(z_lo * 2, 2)]
         bytes_of(shards, w_recv.at[q])
         remote(shards, shards, wz_send, wz_recv.at[q], at_mate).start()
 
+    def forward(q):
+        forward_g(q)
+        forward_w(q)
+
     forward(0)
-
     @pl.when(down)
     def _():
         vh_up.wait_recv()
@@ -225,33 +244,80 @@
 
     turn(vhalo[...].astype(F32).reshape(128, 128), 8)
 
-    def reduce_z(q):
+    def sum_of(ref):
+        value = ref[0].astype(F32)
+        for k in range(1, 8):
+            value = value + ref[k].astype(F32)
+        return value.astype(BF16)
+
+    def reduce_first(q):
         bytes_of(rs_in.at[q], rs_recv.at[q])
-        for qb in range(QB):
-            rows = slice(80 * qb, 80 * qb + 80)
-            value = rs_in[q, 0, rows].astype(F32)
-            for zs in range(1, 8):
-                value = value + rs_in[q, zs, rows].astype(F32)
-            a_out[q, qb] = value.astype(BF16)
-            for u in range(2):
-                piece = a_out.at[q, qb, 32 * u : 32 * u + 48]
-                to = 2 * (q * QB + qb) + u
-
-                @pl.when(y == to)
-                def _():
-                    local(piece, a_in.at[y], a_recv).start()
-
-                @pl.when(y != to)
-                def _():
-                    remote(piece, a_in.at[y], a_send, a_recv, place(x, to, z, c)).start()
-
-    def step(q, _):
-        @pl.when(q < NQ - 1)
-        def _():
-            forward(q + 1)
-
-        bytes_of(gbuf.at[q, :, 1 - c, 64:576], p_recv.at[q])
-        bytes_of(wbuf.at[q, :, pl.ds((1 - z_lo) * 2, 2)], wz_recv.at[q])
+        a_out[q] = sum_of(rs_in.at[q])
+
+        @pl.when(sums_y)
+        def _():
+            local(a_out.at[q], a_in.at[q, y], a_recv.at[q]).start()
+
+        @pl.when(jnp.logical_not(sums_y))
+        def _():
+            remote(a_out.at[q], a_in.at[q, y], a_send, a_recv.at[q], place(x, block, z, c)).start()
+
+        bytes_of(ry_in.at[q], ry_recv.at[q])
+        ay_out[q] = sum_of(ry_in.at[q])
+        z_to = 2 * q + div(y, 4)
+
+        @pl.when(z_to == z)
+        def _():
+            local(ay_out.at[q], ay_in.at[z], ay_recv).start()
+
+        @pl.when(z_to != z)
+        def _():
+            remote(ay_out.at[q], ay_in.at[z], ay_send, ay_recv, place(x, y, z_to, c)).start()
+
+    def reduce_last_z():
+        @pl.when(sums_z)
+        def _():
+            bytes_of(ay_in, ay_recv)
+            cy_out[...] = sum_of(ay_in)
+
+            @pl.when(own_y)
+            def _():
+                local(cy_out, cy_in.at[half_y], cy_recv).start()
+
+            @pl.when(jnp.logical_not(own_y))
+            def _():
+                remote(cy_out, cy_in.at[half_y], cy_send, cy_recv, place(x, block, z, core_y)).start()
+
+            for k in range(1, 4):
+                remote(
+                    cy_out, cy_in.at[half_y], cy_send, cy_recv, place(rem(x + k, 4), block, z, core_y)
+                ).start()
+
+    def reduce_y(quarter):
+        @pl.when(sums_y)
+        def _():
+            bytes_of(a_in.at[quarter], a_recv.at[quarter])
+            c_out[quarter] = sum_of(a_in.at[quarter])
+            z_owner = 2 * quarter + z_lo
+            mine = part_own & (z_owner == z)
+
+            @pl.when(mine)
+            def _():
+                local(c_out.at[quarter], c_in.at[part_half], c_recv).start()
+
+            @pl.when(jnp.logical_not(mine))
+            def _():
+                remote(
+                    c_out.at[quarter], c_in.at[part_half], c_send, c_recv, place(x, y, z_owner, part_core)
+                ).start()
+
+            for k in range(1, 4):
+                remote(
+                    c_out.at[quarter], c_in.at[part_half], c_send, c_recv,
+                    place(rem(x + k, 4), y, z_owner, part_core),
+                ).start()
+
+    def gather(q):
         kern = wbuf[q].reshape(192, 3 * LANES)
         windows = []
         for arr in range(2):
@@ -271,34 +337,69 @@
                         )
                     )
             windows.append(jnp.concatenate(views, axis=0))
+        return kern, windows
+
+    def back(q, kern, windows):
+        for arr, factor in ((0, kern), (1, jnp.abs(kern))):
+            acc[arr, :, 0:192] += lax.dot_general(
+                windows[arr], factor, (((1,), (1,)), ((), ())), preferred_element_type=F32
+            )
+
+    def step(q, _):
+        @pl.when(q < NQ - 1)
+        def _():
+            forward_w(q + 1)
+
+        bytes_of(gbuf.at[q, :, 1 - c, 64:576], p_recv.at[q])
+        bytes_of(wbuf.at[q, :, pl.ds((1 - z_lo) * 2, 2)], wz_recv.at[q])
+        kern, windows = gather(q)
         terms = [jnp.dot(vt[arr], windows[arr], preferred_element_type=F32) for arr in range(2)]
         wide = kern.astype(F32)
         signed = jnp.where(wide > 0, terms[1], jnp.where(wide < 0, -terms[1], 0.0))
         partial = (terms[0] + signed).astype(BF16)
-        for zd in range(8):
-            shard, half = (zd % 2) * 2 + zd // 4, (zd // 2) % 2
-            for qb in range(QB):
-                for k in range(5):
-                    a, tap = divmod(4 * half + k, 3)
-                    rs_out[q, zd, 80 * qb + 16 * k : 80 * qb + 16 * k + 16, :] = partial[
-                        tap * 64 + shard * 16 : tap * 64 + shard * 16 + 16,
-                        a * LANES + 128 * qb : a * LANES + 128 * qb + 128,
-                    ]
+
+        def tile(tap_at, shard):
+            a, tap = divmod(tap_at, 3)
+            return partial[
+                tap * 64 + shard * 16 : tap * 64 + shard * 16 + 16, a * 128 : a * 128 + 128
+            ]
+
+        for to in range(8):
+            for k in range(3):
+                rs_out[q, to, 16 * k : 16 * k + 16, :] = tile(2 * ((to // 2) % 2) + k, (to % 2) * 2 + to // 4)
         local(rs_out.at[q, z], rs_in.at[q, z], rs_recv.at[q]).start()
         for k in range(1, 8):
             zd = rem(z + k, 8)
             remote(rs_out.at[q, zd], rs_in.at[q, z], rs_send, rs_recv.at[q], place(x, y, zd, c)).start()
-        for arr, factor in ((0, kern), (1, jnp.abs(kern))):
-            acc[arr, :, 0:192] += lax.dot_general(
-                windows[arr], factor, (((1,), (1,)), ((), ())), preferred_element_type=F32
-            )
+        for to in range(8):
+            for k in range(2):
+                ry_out[q, to, 16 * k : 16 * k + 16, :] = tile(5 + 2 * (to % 2) + k, to // 2)
+        local(ry_out.at[q, y], ry_in.at[q, y], ry_recv.at[q]).start()
+        for k in range(1, 8):
+            yd = rem(y + k, 8)
+            remote(ry_out.at[q, yd], ry_in.at[q, y], ry_send, ry_recv.at[q], place(x, yd, z, c)).start()
+
+        @pl.when(q < NQ - 1)
+        def _():
+            forward_g(q + 1)
+
+        back(q, kern, windows)
 
         @pl.when(q > 0)
         def _():
-            reduce_z(q - 1)
+            reduce_first(q - 1)
+
+        @pl.when(q > 1)
+        def _():
+            reduce_y(q - 2)
         return 0
 
     lax.fori_loop(0, NQ, step, 0)
+
+    def late(q, _):
+        back(q, *gather(q))
+        return 0
+
 
     column64 = lax.broadcasted_iota(jnp.int32, (64, 128), 0) & 31
     low64 = lax.broadcasted_iota(jnp.int32, (64, 128), 1) < 64
@@ -352,7 +453,8 @@
 
     for b in (1, 2, 5, 6):
         r_start(b)
-    reduce_z(NQ - 1)
+    reduce_y(NQ - 2)
+    reduce_first(NQ - 1)
 
     @pl.when(up)
     def _():
@@ -369,25 +471,8 @@
     for b in (0, 3, 4, 7):
         r_start(b)
 
-    bytes_of(a_in, a_recv)
-    value = a_in[0].astype(F32)
-    for ys in range(1, 8):
-        value = value + a_in[ys].astype(F32)
-    c_out[...] = value.astype(BF16)
-    slot = c_in.at[2 * part_half + u_own]
-
-    @pl.when(own_part)
-    def _():
-        local(c_out, slot, c_recv).start()
-
-    @pl.when(jnp.logical_not(own_part))
-    def _():
-        remote(c_out, slot, c_send, c_recv, place(x, block, 2 * q_own + z_lo, part_core)).start()
-
-    for k in range(1, 4):
-        remote(
-            c_out, slot, c_send, c_recv, place(rem(x + k, 4), block, 2 * q_own + z_lo, part_core)
-        ).start()
+    reduce_y(NQ - 1)
+    reduce_last_z()
 
     bytes_of(r_in, r_recv)
     for j in range(4):
@@ -395,11 +480,7 @@
         even, odd = r_in[2 * j].astype(F32), r_in[2 * j + 1].astype(F32)
         center = jnp.where(low, even, pltpu.roll(odd, 64, 1))
         radius = jnp.where(low, pltpu.roll(even, 64, 1), odd)
-        middle, spread = cm[:, lanes].astype(F32), rm[:, lanes].astype(F32)
-        upper = jnp.where(middle > -spread, 0.5 * (center + radius), 0.0)
-        lower = jnp.where(middle > spread, 0.5 * (center - radius), 0.0)
-        cm_out[:, lanes] = (upper + lower).astype(BF16)
-        rm_out[:, lanes] = (upper - lower).astype(BF16)
+        cm_out[:, lanes], rm_out[:, lanes] = center.astype(BF16), radius.astype(BF16)
 
     bytes_of(vsend.at[0:7], v_send)
     bytes_of(r_in.at[0:7], r_send)
@@ -427,23 +508,42 @@
         bytes_of(acc.at[0], w_send)
 
     bytes_of(rs_out.at[:, 0:7], rs_send)
-    bytes_of(a_in.at[0:7], a_send)
-
-    @pl.when(own_part)
-    def _():
-        bytes_of(c_in.at[0:3], c_send)
-
-    @pl.when(jnp.logical_not(own_part))
-    def _():
-        bytes_of(c_in, c_send)
+    bytes_of(ry_out.at[:, 0:7], ry_send)
+
+    @pl.when(jnp.logical_not(sums_y))
+    def _():
+        bytes_of(a_out, a_send)
+
+    @pl.when(sums_z)
+    def _():
+        bytes_of(ay_out.at[0:3], ay_send)
+
+    @pl.when(jnp.logical_not(sums_z))
+    def _():
+        bytes_of(ay_out, ay_send)
+
+    @pl.when(sums_z & own_y)
+    def _():
+        bytes_of(ay_in.at[0:3], cy_send)
+
+    @pl.when(sums_z & jnp.logical_not(own_y))
+    def _():
+        bytes_of(ay_in.at[0:4], cy_send)
+
+    @pl.when(sums_y & part_own)
+    def _():
+        bytes_of(a_in.at[0:3, 0:5], c_send)
+
+    @pl.when(sums_y & jnp.logical_not(part_own))
+    def _():
+        bytes_of(a_in.at[0:2], c_send)
 
     bytes_of(c_in, c_recv)
-    for half in range(2):
-        for u in range(2):
-            first = 0 if half == u == 0 else 1
-            wg_out[64 * half + 32 * u + 16 * first : 64 * half + 32 * u + 48, :] = (
-                c_in[2 * half + u, 16 * first : 48, :].astype(F32) * (1.0 / 32.0)
-            )
+    bytes_of(cy_in, cy_recv)
+    for rows, value in (
+        ((0, 48), c_in[0]), ((48, 80), c_in[1, 16:48]), ((80, 112), cy_in[0]), ((112, 144), cy_in[1]),
+    ):
+        wg_out[rows[0] : rows[1], :] = value.astype(F32) * (1.0 / 32.0)
 
 
 def on_device(center_mid, radius_mid, conv_weight, center_upstream, radius_upstream):
@@ -451,7 +551,7 @@
     weight = conv_weight.reshape(16, 3, 3, NQ, LANES).transpose(3, 2, 0, 1, 4)
     weight = weight.reshape(NQ, 3, 16, 3 * LANES)
     dma = pltpu.SemaphoreType.DMA
-    hbm, vmem = pl.BlockSpec(memory_space=pl.ANY), pl.BlockSpec(memory_space=pltpu.VMEM)
+    hbm, vmem = pl.BlockSpec(memory_space=pltpu.HBM), pl.BlockSpec(memory_space=pltpu.VMEM)
     center_grad, radius_grad, weight_grad = pl.pallas_call(
         kernel,
         out_shape=(
@@ -471,25 +571,37 @@
             pltpu.VMEM((NQ, 2, 2, 640, LANES), BF16),
             pltpu.VMEM((NQ, 3, 4, 16, 3 * LANES), BF16),
             pltpu.VMEM((2, 1152, 256), F32),
-            pltpu.VMEM((NQ, 8, 80 * QB, 128), BF16),
-            pltpu.VMEM((NQ, 8, 80 * QB, 128), BF16),
-            pltpu.VMEM((NQ, QB, 80, 128), BF16),
-            pltpu.VMEM((8, 48, 128), BF16),
-            pltpu.VMEM((48, 128), BF16),
+            pltpu.VMEM((4, 8, 48, 128), BF16),
+            pltpu.VMEM((4, 8, 48, 128), BF16),
+            pltpu.VMEM((4, 8, 32, 128), BF16),
+            pltpu.VMEM((4, 8, 32, 128), BF16),
             pltpu.VMEM((4, 48, 128), BF16),
+            pltpu.VMEM((4, 8, 48, 128), BF16),
+            pltpu.VMEM((4, 32, 128), BF16),
+            pltpu.VMEM((8, 32, 128), BF16),
+            pltpu.VMEM((4, 48, 128), BF16),
+            pltpu.VMEM((2, 48, 128), BF16),
+            pltpu.VMEM((32, 128), BF16),
+            pltpu.VMEM((2, 32, 128), BF16),
             pltpu.VMEM((2, 2, 32, 128), F32),
             pltpu.VMEM((2, 2, 32, 128), F32),
             pltpu.VMEM((1152, 128), F32),
             pltpu.VMEM((2, 512, 128), BF16),
             pltpu.VMEM((8, 128, 128), BF16),
             dma((2,)), dma((NQ,)), dma, dma, dma((2,)), dma((2,)), dma, dma((NQ,)), dma, dma((NQ,)),
-            dma, dma((NQ,)), dma, dma((NQ,)), dma, dma((NQ,)), dma, dma, dma, dma,
+            dma, dma((NQ,)), dma, dma((NQ,)), dma, dma((NQ,)), dma, dma((NQ,)), dma, dma((4,)), dma, dma,
+            dma, dma, dma, dma,
             dma((2,)), dma((2,)), dma, dma,
         ],
         compiler_params=pltpu.CompilerParams(
             collective_id=0, has_side_effects=True, vmem_limit_bytes=48 << 20
         ),
     )(flat[0], flat[1], flat[2], flat[3], weight)
+    middle, spread = flat[0].astype(F32), flat[1].astype(F32)
+    center, radius = center_grad.astype(F32), radius_grad.astype(F32)
+    upper = jnp.where(middle > -spread, 0.5 * (center + radius), 0.0)
+    lower = jnp.where(middle > spread, 0.5 * (center - radius), 0.0)
+    center_grad, radius_grad = (upper + lower).astype(BF16), (upper - lower).astype(BF16)
     x = lax.rem(lax.axis_index("rows"), 4)
     own = lax.dynamic_slice_in_dim(weight_grad, x * 32, 32, axis=1)
     return (

time: 61.4 us -> 55.6 us (0.906)
  the two profiles are of different devices: /device:TPU:7 before, /device:TPU:17 now
where the time goes in v4:
time: 55.6 us; the launch traced here: 55.4 us
  Pallas kernels  51.1 us (92%)
  local copies, waits for them, and re-layouts  2.79 us (5%)
  other arithmetic  0.85 us (2%)
  between operations  0.7 us (1%)
    pallas_call x1, Pallas kernels, on_device(): pl.pallas_call(kernel, out_shape=(jax.ShapeDtypeStruct((128, 512), BF16),...  51.1 us

profile of v4, /device:TPU:17, one launch (start us, length us, event | category | flops | bytes accessed | tf_op | source)
XLA Modules:
  0.0 55.4 jit_solution(928019119706103231)
XLA Ops:
  0.6 0.9 %reshape.37 = bf16[16,3,3,4,128]{4,3,0,2,1:T(4,128)(2,1)S(1)} reshape(bf16[16,3,3,512]{3,0,2,1:T(8,128)(2,1)} %param.7) | data formatting | bytes 294912 | tf_op jit(solution)/shard_map/reshape | solution.py:551
  1.6 0.0 copy-start.2
  1.6 0.0 copy-start.3
  1.6 0.1 copy.11
  1.8 0.0 copy-start
  1.8 0.0 copy-start.1
  1.8 0.1 reshape.38.w_ref
  1.9 0.6 %copy-done.2 = bf16[1,4,32,512]{3,2,1,0:T(8,128)(2,1)S(1)} copy-done((bf16[1,4,32,512]{3,2,1,0:T(8,128)(2,1)S(1)}, bf16[1,4,32,512]{3,2,1,0:T(8,128)(2,1)}, u32[]{:S(2)}) %copy-start.2) | copy-done | bytes 131096
  2.5 0.1 copy-done.3
  2.6 0.1 copy-done
  2.7 0.1 copy-done.1
  2.8 51.1 %shard_map.76 = (bf16[128,512]{1,0:T(8,128)(2,1)S(1)}, bf16[128,512]{1,0:T(8,128)(2,1)S(1)}, f32[144,128]{1,0:T(8,128)S(1)}) custom-call(bf16[128,512]{1,0:T(8,128)(2,1)S(1)} %bitcast.20, bf16[128,512]{1,0:T(8,128)(2,1)S(1)} %bitcast.21, bf16[128,512]{1,0:T(8,128)(2,1)S(1)} %bitcast.22, bf16[128,512]{1,0:T(8,128)(2,1)S(1)} %bitcast.23, ...), custom_call_target="tpu_custom_call" | custom-call | tf_op jit(solution)/shard_map/pallas_call | solution.py:555
  53.8 0.7 %constant_dynamic-slice_fusion = f32[144,32]{1,0:T(8,128)} fusion(f32[144,128]{1,0:T(8,128)S(1)} %get-tuple-element.8, s32[]{:T(128)S(6)} %select_n.12), kind=kLoop, calls=%fused_computation.12 | loop fusion | bytes 36868 | tf_op jit(solution)/shard_map/dynamic_slice | solution.py:606
  54.6 0.9 %subtract_convert_fusion = (bf16[128,512]{1,0:T(8,128)(2,1)}, bf16[128,512]{1,0:T(8,128)(2,1)}) fusion(bf16[128,512]{1,0:T(8,128)(2,1)S(1)} %get-tuple-element.7, bf16[128,512]{1,0:T(8,128)(2,1)S(1)} %get-tuple-element.6, bf16[1,4,32,512]{3,2,1,0:T(8,128)(2,1)S(1)} %copy-done.1, bf16[1,4,32,512]{3,2,1,0:T(8,128)(2,1)S(1)} %copy-done), kind=kLoop, calls=%fused_computation.9 | loop fusion | flops 1114112 | bytes 786432 | tf_op jit(solution)/shard_map/convert_element_type | solution.py:604
Async XLA Ops:
  1.6 0.9 %copy-start.2 = (bf16[1,4,32,512]{3,2,1,0:T(8,128)(2,1)S(1)}, bf16[1,4,32,512]{3,2,1,0:T(8,128)(2,1)}, u32[]{:S(2)}) copy-start(bf16[1,4,32,512]{3,2,1,0:T(8,128)(2,1)} %param.8) | copy-start | bytes 393220
  1.6 1.0 %copy-start.3 = (bf16[1,4,32,512]{3,2,1,0:T(8,128)(2,1)S(1)}, bf16[1,4,32,512]{3,2,1,0:T(8,128)(2,1)}, u32[]{:S(2)}) copy-start(bf16[1,4,32,512]{3,2,1,0:T(8,128)(2,1)} %param.9) | copy-start | bytes 393220
  1.8 0.9 %copy-start = (bf16[1,4,32,512]{3,2,1,0:T(8,128)(2,1)S(1)}, bf16[1,4,32,512]{3,2,1,0:T(8,128)(2,1)}, u32[]{:S(2)}) copy-start(bf16[1,4,32,512]{3,2,1,0:T(8,128)(2,1)} %param.5) | copy-start | bytes 393220
  1.8 1.0 %copy-start.1 = (bf16[1,4,32,512]{3,2,1,0:T(8,128)(2,1)S(1)}, bf16[1,4,32,512]{3,2,1,0:T(8,128)(2,1)}, u32[]{:S(2)}) copy-start(bf16[1,4,32,512]{3,2,1,0:T(8,128)(2,1)} %param.6) | copy-start | bytes 393220

commit v5 on v4

--- a/solution.py
+++ b/solution.py
@@ -8,6 +8,8 @@
 MESH = pl.DeviceIdType.MESH
 F32 = jnp.float32
 BF16 = jnp.bfloat16
+LAG = 2
+FAR = (4, 3, 5, 2, 6, 1, 7)
 NQ = 4
 LANES = 512 // NQ
 QB = 4 // NQ
@@ -71,7 +73,7 @@
     def greet(where):
         pl.semaphore_signal(barrier, inc=1, device_id=where, device_id_type=MESH)
 
-    for k in range(1, 8):
+    for k in FAR:
         greet(place(rem(x + k, 4), y, z, rem(c + k // 4, 2)))
         greet(place(x, y, rem(z + k, 8), c))
         greet(place(x, rem(y + k, 8), z, c))
@@ -125,18 +127,12 @@
 
     pl.semaphore_wait(barrier, expected)
 
-    v_place = vmain.at[c, pl.ds(mul(128 * x, 128), 128)]
-    for k in range(1, 8):
-        xd, cd = rem(x + k, 4), rem(c + k // 4, 2)
-        remote(vsend.at[xd + 4 * cd], v_place, v_send, v_recv, place(xd, y, z, cd)).start()
-    local(vsend.at[block], v_place, v_recv).start()
-
     own_shard = z_lo * 2 + c
 
     def start_w(q):
         @pl.when(w_source)
         def _():
-            for k in range(1, 8):
+            for k in FAR:
                 remote(
                     w_ref.at[q], wbuf.at[q, :, own_shard], w_send, w_recv.at[q],
                     place(x, rem(y + k, 8), z, w_core),
@@ -155,11 +151,18 @@
     def start_g(q):
         own = gbuf.at[q, :, c, own_rows]
         bytes_of(own, gload_sem.at[q])
-        for k in range(1, 4):
+        for k in (2, 1, 3):
             remote(own, own, g_send, g_recv.at[q], place(rem(x + k, 4), y, z, c)).start()
 
+    start_w(0)
+    v_place = vmain.at[c, pl.ds(mul(128 * x, 128), 128)]
+    for k in (2, 6, 1, 3, 5, 7, 4):
+        xd, cd = rem(x + k, 4), rem(c + k // 4, 2)
+        remote(vsend.at[xd + 4 * cd], v_place, v_send, v_recv, place(xd, y, z, cd)).start()
+    local(vsend.at[block], v_place, v_recv).start()
     for q in range(NQ):
-        start_w(q)
+        if q > 0:
+            start_w(q)
         start_g(q)
 
     zero_rows = jnp.zeros((64, LANES), BF16)
@@ -221,11 +224,9 @@
         bytes_of(shards, w_recv.at[q])
         remote(shards, shards, wz_send, wz_recv.at[q], at_mate).start()
 
-    def forward(q):
-        forward_g(q)
-        forward_w(q)
-
-    forward(0)
+    forward_g(0)
+    forward_w(0)
+    forward_w(1)
     @pl.when(down)
     def _():
         vh_up.wait_recv()
@@ -346,9 +347,9 @@
             )
 
     def step(q, _):
-        @pl.when(q < NQ - 1)
-        def _():
-            forward_w(q + 1)
+        @pl.when(q < NQ - 2)
+        def _():
+            forward_w(q + 2)
 
         bytes_of(gbuf.at[q, :, 1 - c, 64:576], p_recv.at[q])
         bytes_of(wbuf.at[q, :, pl.ds((1 - z_lo) * 2, 2)], wz_recv.at[q])
@@ -368,14 +369,14 @@
             for k in range(3):
                 rs_out[q, to, 16 * k : 16 * k + 16, :] = tile(2 * ((to // 2) % 2) + k, (to % 2) * 2 + to // 4)
         local(rs_out.at[q, z], rs_in.at[q, z], rs_recv.at[q]).start()
-        for k in range(1, 8):
+        for k in FAR:
             zd = rem(z + k, 8)
             remote(rs_out.at[q, zd], rs_in.at[q, z], rs_send, rs_recv.at[q], place(x, y, zd, c)).start()
         for to in range(8):
             for k in range(2):
                 ry_out[q, to, 16 * k : 16 * k + 16, :] = tile(5 + 2 * (to % 2) + k, to // 2)
         local(ry_out.at[q, y], ry_in.at[q, y], ry_recv.at[q]).start()
-        for k in range(1, 8):
+        for k in FAR:
             yd = rem(y + k, 8)
             remote(ry_out.at[q, yd], ry_in.at[q, y], ry_send, ry_recv.at[q], place(x, yd, z, c)).start()
 
@@ -385,21 +386,16 @@
 
         back(q, kern, windows)
 
-        @pl.when(q > 0)
-        def _():
-            reduce_first(q - 1)
-
-        @pl.when(q > 1)
-        def _():
-            reduce_y(q - 2)
+        @pl.when(q >= LAG)
+        def _():
+            reduce_first(q - LAG)
+
+        @pl.when(q >= LAG + 1)
+        def _():
+            reduce_y(q - LAG - 1)
         return 0
 
     lax.fori_loop(0, NQ, step, 0)
-
-    def late(q, _):
-        back(q, *gather(q))
-        return 0
-
 
     column64 = lax.broadcasted_iota(jnp.int32, (64, 128), 0) & 31
     low64 = lax.broadcasted_iota(jnp.int32, (64, 128), 1) < 64
@@ -453,8 +449,9 @@
 
     for b in (1, 2, 5, 6):
         r_start(b)
-    reduce_y(NQ - 2)
-    reduce_first(NQ - 1)
+    for q in range(NQ - LAG, NQ):
+        reduce_first(q)
+        reduce_y(q - 1)
 
     @pl.when(up)
     def _():

time: 55.6 us -> 52.3 us (0.941)
  the two profiles are of different devices: /device:TPU:17 before, /device:TPU:8 now
where the time goes in v5:
time: 52.3 us; the launch traced here: 52.1 us
  Pallas kernels  47.8 us (91%)
  local copies, waits for them, and re-layouts  2.79 us (5%)
  other arithmetic  0.85 us (2%)
  between operations  0.7 us (1%)
    pallas_call x1, Pallas kernels, on_device(): pl.pallas_call(kernel, out_shape=(jax.ShapeDtypeStruct((128, 512), BF16),...  47.8 us
    reshape x2, local copies, waits for them, and re-layouts, on_device(): weight = conv_weight.reshape(16, 3, 3, NQ, LANES).transpose(3, 2, 0, 1, 4)  1.08 us

profile of v5, /device:TPU:8, one launch (start us, length us, event | category | flops | bytes accessed | tf_op | source)
XLA Modules:
  0.0 52.1 jit_solution(1726791115841145713)
XLA Ops:
  0.6 0.9 %reshape.37 = bf16[16,3,3,4,128]{4,3,0,2,1:T(4,128)(2,1)S(1)} reshape(bf16[16,3,3,512]{3,0,2,1:T(8,128)(2,1)} %param.7) | data formatting | bytes 294912 | tf_op jit(solution)/shard_map/reshape | solution.py:548
  1.6 0.0 copy-start.2
  1.6 0.0 copy-start.3
  1.6 0.1 copy.11
  1.8 0.0 copy-start
  1.8 0.0 copy-start.1
  1.8 0.1 reshape.38.w_ref
  1.9 0.6 %copy-done.2 = bf16[1,4,32,512]{3,2,1,0:T(8,128)(2,1)S(1)} copy-done((bf16[1,4,32,512]{3,2,1,0:T(8,128)(2,1)S(1)}, bf16[1,4,32,512]{3,2,1,0:T(8,128)(2,1)}, u32[]{:S(2)}) %copy-start.2) | copy-done | bytes 131096
  2.5 0.1 copy-done.3
  2.6 0.1 copy-done
  2.7 0.1 copy-done.1
  2.8 47.8 %shard_map.76 = (bf16[128,512]{1,0:T(8,128)(2,1)S(1)}, bf16[128,512]{1,0:T(8,128)(2,1)S(1)}, f32[144,128]{1,0:T(8,128)S(1)}) custom-call(bf16[128,512]{1,0:T(8,128)(2,1)S(1)} %bitcast.20, bf16[128,512]{1,0:T(8,128)(2,1)S(1)} %bitcast.21, bf16[128,512]{1,0:T(8,128)(2,1)S(1)} %bitcast.22, bf16[128,512]{1,0:T(8,128)(2,1)S(1)} %bitcast.23, ...), custom_call_target="tpu_custom_call" | custom-call | tf_op jit(solution)/shard_map/pallas_call | solution.py:552
  50.5 0.7 %constant_dynamic-slice_fusion = f32[144,32]{1,0:T(8,128)} fusion(f32[144,128]{1,0:T(8,128)S(1)} %get-tuple-element.8, s32[]{:T(128)S(6)} %select_n.12), kind=kLoop, calls=%fused_computation.12 | loop fusion | bytes 36868 | tf_op jit(solution)/shard_map/dynamic_slice | solution.py:603
  51.3 0.9 %subtract_convert_fusion = (bf16[128,512]{1,0:T(8,128)(2,1)}, bf16[128,512]{1,0:T(8,128)(2,1)}) fusion(bf16[128,512]{1,0:T(8,128)(2,1)S(1)} %get-tuple-element.7, bf16[128,512]{1,0:T(8,128)(2,1)S(1)} %get-tuple-element.6, bf16[1,4,32,512]{3,2,1,0:T(8,128)(2,1)S(1)} %copy-done.1, bf16[1,4,32,512]{3,2,1,0:T(8,128)(2,1)S(1)} %copy-done), kind=kLoop, calls=%fused_computation.9 | loop fusion | flops 1114112 | bytes 786432 | tf_op jit(solution)/shard_map/convert_element_type | solution.py:601
Async XLA Ops:
  1.6 0.9 %copy-start.2 = (bf16[1,4,32,512]{3,2,1,0:T(8,128)(2,1)S(1)}, bf16[1,4,32,512]{3,2,1,0:T(8,128)(2,1)}, u32[]{:S(2)}) copy-start(bf16[1,4,32,512]{3,2,1,0:T(8,128)(2,1)} %param.8) | copy-start | bytes 393220
  1.6 1.0 %copy-start.3 = (bf16[1,4,32,512]{3,2,1,0:T(8,128)(2,1)S(1)}, bf16[1,4,32,512]{3,2,1,0:T(8,128)(2,1)}, u32[]{:S(2)}) copy-start(bf16[1,4,32,512]{3,2,1,0:T(8,128)(2,1)} %param.9) | copy-start | bytes 393220
  1.8 0.9 %copy-start = (bf16[1,4,32,512]{3,2,1,0:T(8,128)(2,1)S(1)}, bf16[1,4,32,512]{3,2,1,0:T(8,128)(2,1)}, u32[]{:S(2)}) copy-start(bf16[1,4,32,512]{3,2,1,0:T(8,128)(2,1)} %param.5) | copy-start | bytes 393220
  1.8 1.0 %copy-start.1 = (bf16[1,4,32,512]{3,2,1,0:T(8,128)(2,1)S(1)}, bf16[1,4,32,512]{3,2,1,0:T(8,128)(2,1)}, u32[]{:S(2)}) copy-start(bf16[1,4,32,512]{3,2,1,0:T(8,128)(2,1)} %param.6) | copy-start | bytes 393220

commit v6 on v5

--- a/solution.py
+++ b/solution.py
@@ -368,17 +368,15 @@
         for to in range(8):
             for k in range(3):
                 rs_out[q, to, 16 * k : 16 * k + 16, :] = tile(2 * ((to // 2) % 2) + k, (to % 2) * 2 + to // 4)
-        local(rs_out.at[q, z], rs_in.at[q, z], rs_recv.at[q]).start()
-        for k in FAR:
-            zd = rem(z + k, 8)
-            remote(rs_out.at[q, zd], rs_in.at[q, z], rs_send, rs_recv.at[q], place(x, y, zd, c)).start()
         for to in range(8):
             for k in range(2):
                 ry_out[q, to, 16 * k : 16 * k + 16, :] = tile(5 + 2 * (to % 2) + k, to // 2)
+        for k in FAR:
+            zd, yd = rem(z + k, 8), rem(y + k, 8)
+            remote(rs_out.at[q, zd], rs_in.at[q, z], rs_send, rs_recv.at[q], place(x, y, zd, c)).start()
+            remote(ry_out.at[q, yd], ry_in.at[q, y], ry_send, ry_recv.at[q], place(x, yd, z, c)).start()
+        local(rs_out.at[q, z], rs_in.at[q, z], rs_recv.at[q]).start()
         local(ry_out.at[q, y], ry_in.at[q, y], ry_recv.at[q]).start()
-        for k in FAR:
-            yd = rem(y + k, 8)
-            remote(ry_out.at[q, yd], ry_in.at[q, y], ry_send, ry_recv.at[q], place(x, yd, z, c)).start()
 
         @pl.when(q < NQ - 1)
         def _():

time: 52.3 us -> 52.2 us (level)
  no operation moved by 1% of the time
where the time goes in v6:
time: 52.2 us; the launch traced here: 52 us
  Pallas kernels  47.7 us (91%)
  local copies, waits for them, and re-layouts  2.79 us (5%)
  other arithmetic  0.85 us (2%)
  between operations  0.7 us (1%)
    pallas_call x1, Pallas kernels, on_device(): pl.pallas_call(kernel, out_shape=(jax.ShapeDtypeStruct((128, 512), BF16),...  47.7 us
    reshape x2, local copies, waits for them, and re-layouts, on_device(): weight = conv_weight.reshape(16, 3, 3, NQ, LANES).transpose(3, 2, 0, 1, 4)  1.08 us

profile of v6, /device:TPU:8, one launch (start us, length us, event | category | flops | bytes accessed | tf_op | source)
XLA Modules:
  0.0 52.0 jit_solution(14497917281744731624)
XLA Ops:
  0.6 0.9 %reshape.37 = bf16[16,3,3,4,128]{4,3,0,2,1:T(4,128)(2,1)S(1)} reshape(bf16[16,3,3,512]{3,0,2,1:T(8,128)(2,1)} %param.7) | data formatting | bytes 294912 | tf_op jit(solution)/shard_map/reshape | solution.py:546
  1.6 0.0 copy-start.2
  1.6 0.0 copy-start.3
  1.6 0.1 copy.11
  1.8 0.0 copy-start
  1.8 0.0 copy-start.1
  1.8 0.1 reshape.38.w_ref
  1.9 0.6 %copy-done.2 = bf16[1,4,32,512]{3,2,1,0:T(8,128)(2,1)S(1)} copy-done((bf16[1,4,32,512]{3,2,1,0:T(8,128)(2,1)S(1)}, bf16[1,4,32,512]{3,2,1,0:T(8,128)(2,1)}, u32[]{:S(2)}) %copy-start.2) | copy-done | bytes 131096
  2.5 0.1 copy-done.3
  2.6 0.1 copy-done
  2.7 0.1 copy-done.1
  2.8 47.7 %shard_map.76 = (bf16[128,512]{1,0:T(8,128)(2,1)S(1)}, bf16[128,512]{1,0:T(8,128)(2,1)S(1)}, f32[144,128]{1,0:T(8,128)S(1)}) custom-call(bf16[128,512]{1,0:T(8,128)(2,1)S(1)} %bitcast.20, bf16[128,512]{1,0:T(8,128)(2,1)S(1)} %bitcast.21, bf16[128,512]{1,0:T(8,128)(2,1)S(1)} %bitcast.22, bf16[128,512]{1,0:T(8,128)(2,1)S(1)} %bitcast.23, ...), custom_call_target="tpu_custom_call" | custom-call | tf_op jit(solution)/shard_map/pallas_call | solution.py:550
  50.4 0.7 %constant_dynamic-slice_fusion = f32[144,32]{1,0:T(8,128)} fusion(f32[144,128]{1,0:T(8,128)S(1)} %get-tuple-element.8, s32[]{:T(128)S(6)} %select_n.12), kind=kLoop, calls=%fused_computation.12 | loop fusion | bytes 36868 | tf_op jit(solution)/shard_map/dynamic_slice | solution.py:601
  51.2 0.9 %subtract_convert_fusion = (bf16[128,512]{1,0:T(8,128)(2,1)}, bf16[128,512]{1,0:T(8,128)(2,1)}) fusion(bf16[128,512]{1,0:T(8,128)(2,1)S(1)} %get-tuple-element.7, bf16[128,512]{1,0:T(8,128)(2,1)S(1)} %get-tuple-element.6, bf16[1,4,32,512]{3,2,1,0:T(8,128)(2,1)S(1)} %copy-done.1, bf16[1,4,32,512]{3,2,1,0:T(8,128)(2,1)S(1)} %copy-done), kind=kLoop, calls=%fused_computation.9 | loop fusion | flops 1114112 | bytes 786432 | tf_op jit(solution)/shard_map/convert_element_type | solution.py:599
Async XLA Ops:
  1.6 0.9 %copy-start.2 = (bf16[1,4,32,512]{3,2,1,0:T(8,128)(2,1)S(1)}, bf16[1,4,32,512]{3,2,1,0:T(8,128)(2,1)}, u32[]{:S(2)}) copy-start(bf16[1,4,32,512]{3,2,1,0:T(8,128)(2,1)} %param.8) | copy-start | bytes 393220
  1.6 1.0 %copy-start.3 = (bf16[1,4,32,512]{3,2,1,0:T(8,128)(2,1)S(1)}, bf16[1,4,32,512]{3,2,1,0:T(8,128)(2,1)}, u32[]{:S(2)}) copy-start(bf16[1,4,32,512]{3,2,1,0:T(8,128)(2,1)} %param.9) | copy-start | bytes 393220
  1.8 0.9 %copy-start = (bf16[1,4,32,512]{3,2,1,0:T(8,128)(2,1)S(1)}, bf16[1,4,32,512]{3,2,1,0:T(8,128)(2,1)}, u32[]{:S(2)}) copy-start(bf16[1,4,32,512]{3,2,1,0:T(8,128)(2,1)} %param.5) | copy-start | bytes 393220
  1.8 1.0 %copy-start.1 = (bf16[1,4,32,512]{3,2,1,0:T(8,128)(2,1)S(1)}, bf16[1,4,32,512]{3,2,1,0:T(8,128)(2,1)}, u32[]{:S(2)}) copy-start(bf16[1,4,32,512]{3,2,1,0:T(8,128)(2,1)} %param.6) | copy-start | bytes 393220
